TPU v7x, 128 devices: a whole 4x4x4 slice. The times are simulated.
128 devices in a mesh: dp: 8 (over z, core), expert: 16 (over y, x).
Axes of the slice: x: 4, y: 4, z: 4, core: 2. Of those that a mesh axis runs over, the one named last changes fastest.
Arguments:
- queries: bfloat16 [2048, 64, 576], P('dp', 'expert'), may hold values from -6 to 6
- cached_latent_rows: bfloat16 [2048, 8, 576], P('dp'), may hold values from -6 to 6
- lengths: int32 [2048], P('dp'), may hold values from 1 to 8, 8192 in all
- value_up_weight: bfloat16 [64, 512, 128], P('expert'), may hold values from -0.25 to 0.25
- out_proj: bfloat16 [8192, 3584], P('expert', 'dp'), may hold values from -0.0625 to 0.0625
- residual_in: bfloat16 [2048, 3584], P(('dp', 'expert')), may hold values from -6 to 6
- norm_gain: float32 [3584], replicated, may hold values from 0.25 to 1.75
- routes: int32 [2048, 8], P(('dp', 'expert')), may hold values from 0 to 127, all different within a row; in each aligned block of 16 rows (0 to 15, 16 to 31, ...) at most 2 rows name the same one
- route_scores: float32 [2048, 8], P(('dp', 'expert')), may hold values from 0.05 to 1
- w_gate_up: bfloat16 [128, 3584, 2048], P(('dp', 'expert')), may hold values from -0.09375 to 0.09375
- w_down: bfloat16 [128, 1024, 3584], P(('dp', 'expert')), may hold values from -0.1875 to 0.1875
Outputs:
- layer_out: bfloat16 [2048, 3584], P(('dp', 'expert'))
Inputs may be any that keep to these rules, and one draw needn't show every extreme that they name: `routes`: the 8 experts of a request differ; among the 16 requests of one device (aligned blocks of rows) no expert is named more than 2 times, a bound that some block reaches.
All inputs are finite; a program needn't handle non-finite values. No bound on the sum of `lengths` on one device may be relied on, other than what follows from the above.
Results may differ from a plain program's by a relative error of at most 0.022.
Values may be sent and summed in bfloat16 or wider, within the bound.
No kernel may reach another device: no remote copies, remote signals or barrier semaphores. Data moves between devices by JAX's collectives and lax.ppermute only.
A program may use at most 128 MiB of HBM per device.

v0:
```python
import jax
import jax.numpy as jnp
from jax import lax
from jax.sharding import PartitionSpec as P

D = 3584
FF = 1024
LATENT_WIDTH = 512
VALUE_HEAD_WIDTH = 128
TOP = 8


score_scale = 0.07216878364870323


def local(
    queries,
    cached_latent_rows,
    lengths,
    value_up_weight,
    out_proj,
    residual_in,
    norm_gain,
    routes,
    route_scores,
    w_gate_up,
    w_down,
):
    requests, heads, width = queries.shape
    length = cached_latent_rows.shape[1]
    full_proj = lax.all_gather(out_proj, "dp", axis=1, tiled=True)
    scores = (
        jnp.einsum("thc,tsc->ths", queries, cached_latent_rows, preferred_element_type=jnp.float32)
        * score_scale
    )
    position = lax.broadcasted_iota(jnp.int32, (1, 1, length), 2)
    scores = jnp.where(position < lengths[:, None, None], scores, jnp.float32(-1e30))
    peak = jnp.max(scores, axis=2, keepdims=True)
    expo = jnp.exp(scores - peak)
    attention_probabilities = (expo / jnp.sum(expo, axis=2, keepdims=True)).astype(jnp.bfloat16)
    latent_output = jnp.einsum(
        "ulj,ujv->ulv",
        attention_probabilities,
        cached_latent_rows[:, :, :LATENT_WIDTH],
        preferred_element_type=jnp.float32,
    ).astype(jnp.bfloat16)
    head_out = jnp.einsum(
        "thc,hcv->thv", latent_output, value_up_weight, preferred_element_type=jnp.float32
    ).astype(jnp.bfloat16)
    flat_heads = head_out.reshape(requests, heads * VALUE_HEAD_WIDTH)
    attention = lax.psum_scatter(
        jnp.dot(flat_heads, full_proj, preferred_element_type=jnp.float32).astype(jnp.bfloat16),
        "expert",
        scatter_dimension=0,
        tiled=True,
    )
    hidden = (residual_in.astype(jnp.float32) + attention.astype(jnp.float32)).astype(jnp.bfloat16)
    hidden_f = hidden.astype(jnp.float32)
    inverse = lax.rsqrt(jnp.mean(hidden_f * hidden_f, axis=1, keepdims=True) + 1e-06)
    normed = (hidden_f * inverse * norm_gain[None, :]).astype(jnp.bfloat16)
    gates = 2.5 * route_scores / jnp.sum(route_scores, axis=1, keepdims=True)
    local_rows = routes.shape[0]
    experts_all = lax.axis_size("dp") * lax.axis_size("expert")
    slots_each = max(2, 2 * local_rows * TOP // experts_all)
    flat_routes = routes.reshape(-1)
    onehot = (flat_routes[:, None] == lax.broadcasted_iota(jnp.int32, (1, experts_all), 1)).astype(
        jnp.int32
    )
    earlier = jnp.cumsum(onehot, axis=0) - onehot
    slot = jnp.sum(onehot * earlier, axis=1)
    target = flat_routes * slots_each + slot
    selector = (
        target[:, None] == lax.broadcasted_iota(jnp.int32, (1, experts_all * slots_each), 1)
    ).astype(jnp.bfloat16)
    normed_rows = jnp.repeat(normed, TOP, axis=0)
    outgoing = jnp.einsum(
        "rk,rd->kd", selector, normed_rows, preferred_element_type=jnp.float32
    ).astype(jnp.bfloat16)
    outgoing = outgoing.reshape(experts_all, slots_each, D)
    arrived = lax.all_to_all(outgoing, ("dp", "expert"), split_axis=0, concat_axis=0, tiled=True)
    flat_in = arrived.reshape(experts_all * slots_each, D)
    both = jnp.dot(flat_in, w_gate_up[0], preferred_element_type=jnp.float32)
    act = (jax.nn.silu(both[:, :FF]) * both[:, FF:]).astype(jnp.bfloat16)
    result = jnp.dot(act, w_down[0], preferred_element_type=jnp.float32).astype(jnp.bfloat16)
    produced = result.reshape(experts_all, slots_each, D)
    returned = lax.all_to_all(produced, ("dp", "expert"), split_axis=0, concat_axis=0, tiled=True)
    returned = returned.reshape(experts_all * slots_each, D)
    picked = jnp.dot(selector, returned, preferred_element_type=jnp.float32)
    picked = picked.reshape(local_rows, TOP, D)
    moe_sum = jnp.sum(picked * gates[:, :, None], axis=1)
    return (hidden_f + moe_sum).astype(jnp.bfloat16)


def solution(mesh):
    in_specs = (
        P("dp", "expert", None),
        P("dp", None, None),
        P("dp"),
        P("expert", None, None),
        P("expert", "dp"),
        P(("dp", "expert"), None),
        P(),
        P(("dp", "expert"), None),
        P(("dp", "expert"), None),
        P(("dp", "expert"), None, None),
        P(("dp", "expert"), None, None),
    )
    out_specs = P(("dp", "expert"), None)
    return jax.shard_map(local, mesh=mesh, in_specs=in_specs, out_specs=out_specs, check_vma=False)
```

profile of v0, /device:TPU:1, one launch (start us, length us, event | category | flops | bytes accessed | tf_op | source)
XLA Modules:
  0.0 224.7 jit_solution(12866695961111828759)
XLA Ops:
  6.5 0.7 all-gather.2.cloned.1.call-update
  7.3 4.9 %copy.19 = bf16[256,8,576]{2,1,0:T(8,128)(2,1)} copy(bf16[256,8,576]{0,2,1:T(8,128)(2,1)} %param.12) | data formatting | bytes 4718592 | tf_op args[1]
  12.2 3.5 %copy.18 = bf16[256,4,576]{2,1,0:T(4,128)(2,1)} copy(bf16[256,4,576]{0,2,1:T(8,128)(2,1)} %param.11) | data formatting | bytes 2359296 | tf_op args[0]
  15.7 3.2 %copy.24 = bf16[256,8,512]{2,1,0:T(8,128)(2,1)} copy(bf16[256,8,512]{0,2,1:T(8,128)(2,1)S(1)} %slice-done) | data formatting | bytes 4194304 | tf_op jit(solution)/shard_map/slice | solution.py:44
  19.0 3.9 %fusion.11 = f32[256,4,8]{2,1,0:T(4,128)S(1)} fusion(bf16[256,4,576]{2,1,0:T(4,128)(2,1)} %copy.18, bf16[256,8,576]{2,1,0:T(8,128)(2,1)} %copy.19, pred[256,8]{1,0:T(8,128)(4,1)S(1)} %iota_compare_fusion.2), kind=kOutput, calls=%fused_computation.14 | convolution fusion | flops 9453568 | bytes 3573760 | tf_op jit(solution)/shard_map/thc,tsc->ths/dot_general | solution.py:33
  23.6 4.7 %fusion.17 = bf16[256,4,512]{2,1,0:T(4,128)(2,1)} fusion(bf16[256,8,512]{2,1,0:T(8,128)(2,1)S(1)} %copy-done.1, f32[256,4]{1,0:T(8,128)S(1)} %fusion.29, f32[256,4,8]{2,1,0:T(4,128)S(1)} %fusion.11), kind=kOutput, calls=%fused_computation.25 | convolution fusion | flops 8414215 | bytes 3182592 | tf_op jit(solution)/shard_map/ulj,ujv->ulv/dot_general | solution.py:41
  28.3 1.7 convolution_convert_fusion.2
  30.0 12.8 %all-gather.2.cloned.1.call-done = bf16[512,3584]{0,1:T(8,128)(2,1)} async-done(((bf16[512,448]{0,1:T(8,128)(2,1)}), bf16[512,3584]{0,1:T(8,128)(2,1)}) %all-gather.2.cloned.1.call-update) | async-done | bytes 3670032 | tf_op jit(solution)/shard_map/all_gather | solution.py:31
  42.9 4.5 %convolution_convert_fusion.1 = bf16[256,3584]{1,0:T(8,128)(2,1)} fusion(bf16[256,512]{0,1:T(8,128)(2,1)S(1)} %bitcast.27, bf16[512,3584]{0,1:T(8,128)(2,1)} %all-gather.2.cloned.1.call-done), kind=kOutput, calls=%fused_computation.7 | convolution fusion | flops 940441600 | bytes 5767168 | tf_op jit(solution)/shard_map/dot_general | solution.py:52
  48.0 71.2 %reduce-scatter.2.cloned.1.call-done = bf16[16,3584]{1,0:T(8,128)(2,1)} async-done(((bf16[256,3584]{1,0:T(8,128)(2,1)}), bf16[16,3584]{1,0:T(8,128)(2,1)}) %reduce-scatter.2.cloned.1.call-update) | async-done | bytes 114704 | tf_op jit(solution)/shard_map/reduce_scatter | solution.py:51
  119.2 1.0 fusion.19
  120.2 1.0 fusion.21
  121.2 2.0 convolution_convert_fusion
  123.2 3.9 %reshape.89 = bf16[128,2,3584]{2,1,0:T(2,128)(2,1)S(1)} reshape(bf16[256,3584]{1,0:T(8,128)(2,1)} %convolution_convert_fusion) | data formatting | bytes 3670016 | tf_op jit(solution)/shard_map/reshape | solution.py:79
  127.1 36.0 %all_to_all.10 = bf16[128,2,3584]{2,1,0:T(2,128)(2,1)} all-to-all(bf16[128,2,3584]{2,1,0:T(2,128)(2,1)S(1)} %reshape.89), channel_id=1, replica_groups=mesh['dp'=8,'expert'=16] {'dp','expert'}, dimensions={0} | all-to-all | bytes 3670016 | tf_op jit(solution)/shard_map/all_to_all | solution.py:80
  163.1 4.1 %reshape.90 = bf16[256,3584]{1,0:T(8,128)(2,1)S(1)} reshape(bf16[128,2,3584]{2,1,0:T(2,128)(2,1)} %all_to_all.10) | data formatting | bytes 3670016 | tf_op jit(solution)/shard_map/reshape | solution.py:81
  167.2 7.3 %fusion.1 = f32[256,2048]{1,0:T(8,128)S(1)} fusion(bf16[256,3584]{1,0:T(8,128)(2,1)S(1)} %reshape.90, bf16[1,3584,2048]{2,1,0:T(8,128)(2,1)} %param.20), kind=kOutput, calls=%fused_computation.1 | convolution fusion | flops 3758096384 | bytes 18612224 | tf_op jit(solution)/shard_map/dot_general | solution.py:82
  174.5 5.2 %fusion.5 = bf16[256,3584]{1,0:T(8,128)(2,1)S(1)} fusion(bf16[1,1024,3584]{2,1,0:T(8,128)(2,1)} %param.21, f32[256,2048]{1,0:T(8,128)S(1)} %fusion.1), kind=kOutput, calls=%fused_computation.5 | convolution fusion | flops 1881538560 | bytes 11272192 | tf_op jit(solution)/shard_map/dot_general | solution.py:84
  179.7 1.7 reshape.91
  181.4 4.8 %all-to-all-start.1 = ((bf16[128,2,3584]{2,1,0:T(2,128)(2,1)}), bf16[128,2,3584]{2,1,0:T(2,128)(2,1)S(1)}, u32[]{:S(2)}, u32[]{:S(2)}) async-start(bf16[128,2,3584]{2,1,0:T(2,128)(2,1)} %reshape.91), calls=%async_computation.2 | async-start | bytes 3670016 | tf_op jit(solution)/shard_map/all_to_all | solution.py:86
  186.4 26.8 %all-to-all-done.1 = bf16[128,2,3584]{2,1,0:T(2,128)(2,1)S(1)} async-done(((bf16[128,2,3584]{2,1,0:T(2,128)(2,1)}), bf16[128,2,3584]{2,1,0:T(2,128)(2,1)S(1)}, u32[]{:S(2)}, u32[]{:S(2)}) %all-to-all-start.1) | async-done | bytes 1835040 | tf_op jit(solution)/shard_map/all_to_all | solution.py:86
  213.2 1.7 reshape.93
  214.9 2.2 fusion.8
  217.1 0.7 fusion.22
  (35 shorter events, 1.6 us)
Async XLA Ops:
  6.5 21.8 %copy-start = (bf16[4,512,128]{2,1,0:T(8,128)(2,1)S(1)}, bf16[4,512,128]{2,1,0:T(8,128)(2,1)}, u32[]{:S(2)}) copy-start(bf16[4,512,128]{2,1,0:T(8,128)(2,1)} %param.14) | copy-start | bytes 1572868
  6.5 36.3 %all-gather.2.cloned.1.call-start = ((), (), s32[]{:S(2)}) async-start(), calls=%async_computation.3 | async-start | bytes 4128768 | tf_op jit(solution)/shard_map/all_gather | solution.py:31
  7.3 111.9 %reduce-scatter.2.cloned.1.call-start = ((), (), s32[]{:S(2)}) async-start(), calls=%async_computation.4 | async-start | bytes 1949696 | tf_op jit(solution)/shard_map/reduce_scatter | solution.py:51
  12.2 3.5 %slice-start = ((bf16[256,8,576]{0,2,1:T(8,128)(2,1)}), bf16[256,8,512]{0,2,1:T(8,128)(2,1)S(1)}, s32[]{:S(2)}) async-start(bf16[256,8,576]{0,2,1:T(8,128)(2,1)} %param.12), calls=%async_computation.5 | async-start | bytes 4194304 | tf_op jit(solution)/shard_map/slice | solution.py:44
  15.7 3.2 %copy-start.7 = (s32[256]{0:T(256)S(1)}, s32[256]{0:T(256)}, u32[]{:S(2)}) copy-start(s32[256]{0:T(256)} %param.13) | copy-start | bytes 3076
  19.0 4.6 %copy-start.1 = (bf16[256,8,512]{2,1,0:T(8,128)(2,1)S(1)}, bf16[256,8,512]{2,1,0:T(8,128)(2,1)}, u32[]{:S(2)}) copy-start(bf16[256,8,512]{2,1,0:T(8,128)(2,1)} %copy.24) | copy-start | bytes 6291460
  42.9 4.5 %copy-start.6 = (s32[16,8]{0,1:T(8,128)S(1)}, s32[16,8]{0,1:T(8,128)}, u32[]{:S(2)}) copy-start(s32[16,8]{0,1:T(8,128)} %param.18) | copy-start | bytes 1540
  47.3 71.8 %copy-start.2 = (bf16[16,3584]{1,0:T(8,128)(2,1)S(1)}, bf16[16,3584]{1,0:T(8,128)(2,1)}, u32[]{:S(2)}) copy-start(bf16[16,3584]{1,0:T(8,128)(2,1)} %param.16) | copy-start | bytes 344068
  47.3 72.9 %copy-start.4 = (f32[3584]{0:T(1024)S(1)}, f32[3584]{0:T(1024)}, u32[]{:S(2)}) copy-start(f32[3584]{0:T(1024)} %param.17) | copy-start | bytes 43012
  181.4 4.9 %copy-start.5 = (f32[16,8]{0,1:T(8,128)S(1)}, f32[16,8]{0,1:T(8,128)}, u32[]{:S(2)}) copy-start(f32[16,8]{0,1:T(8,128)} %param.19) | copy-start | bytes 1540
  181.4 31.8 %all-to-all-start.1 = ((bf16[128,2,3584]{2,1,0:T(2,128)(2,1)}), bf16[128,2,3584]{2,1,0:T(2,128)(2,1)S(1)}, u32[]{:S(2)}, u32[]{:S(2)}) async-start(bf16[128,2,3584]{2,1,0:T(2,128)(2,1)} %reshape.91), calls=%async_computation.2 | async-start | bytes 3670016 | tf_op jit(solution)/shard_map/all_to_all | solution.py:86
  186.4 30.8 %copy-start.3 = (bf16[16,3584]{1,0:T(8,128)(2,1)S(1)}, bf16[16,3584]{1,0:T(8,128)(2,1)}, u32[]{:S(2)}) copy-start(bf16[16,3584]{1,0:T(8,128)(2,1)} %reduce-scatter.2.cloned.1.call-done) | copy-start | bytes 344068
Sparse Core Ops, SparseCore 0:
  9.0 33.7 all-gather.1
  47.5 71.6 reduce-scatter.1
where the time goes:
time: 225 us
  waiting for transfers between devices  112 us (50%)
  blocking collectives  36 us (16%)
  matrix products  31.5 us (14%)
  local copies, waits for them, and re-layouts  23.2 us (10%)
  between operations  13.6 us (6%)
  starting transfers between devices  4.84 us (2%)
  other arithmetic  3.96 us (2%)
    reduce_scatter x1, waiting for transfers between devices, local(): lax.psum_scatter(jnp.dot(flat_heads, full_proj, preferred_element_type=jn...  71.2 us
    all_to_all x1, blocking collectives, local(): lax.all_to_all(outgoing, ('dp', 'expert'), split_axis=0, concat_axis=0, t...  36 us
    all_to_all x1, waiting for transfers between devices, local(): lax.all_to_all(produced, ('dp', 'expert'), split_axis=0, concat_axis=0, t...  26.8 us
    all_gather x1, waiting for transfers between devices, local(): full_proj = lax.all_gather(out_proj, 'dp', axis=1, tiled=True)  12.8 us
    unnamed x19, local copies, waits for them, and re-layouts  8.52 us
    dot_general x1, matrix products, local(): both = jnp.dot(flat_in, w_gate_up[0], preferred_element_type=jnp.float32)  7.26 us
    dot_general x1, matrix products, local(): jnp.dot(act, w_down[0], preferred_element_type=jnp.float32)  5.19 us
    all_to_all x1, starting transfers between devices, local(): lax.all_to_all(produced, ('dp', 'expert'), split_axis=0, concat_axis=0, t...  4.8 us
  transfers between devices with their start and end apart: 3, of which 3 were waited for; matrix products, arithmetic and copies ran while one was open for 10% of the time, Pallas kernels for 0%

commit v1 on v0

v1 whole, which is shorter than its diff:
```python
import functools

import jax
import jax.numpy as jnp
from jax import lax
from jax.experimental import pallas as pl
from jax.experimental.pallas import tpu as pltpu
from jax.sharding import Mesh, PartitionSpec as P

D = 3584
FF = 1024
HEADS = 4
LATENT = 512
WIDTH = 576
VALUE = 128
SLOTS = 8
TOP = 8
EXPERTS = 128
ROWS = 16
REQUESTS = 256
QUARTER = D // 4
PIECES = EXPERTS * 8
COLUMNS = 448

score_scale = 0.07216878364870323

f32, bf16 = jnp.float32, jnp.bfloat16
VMEM_BYTES = 56 * 1024 * 1024


def iota(shape, dim):
    return lax.broadcasted_iota(jnp.int32, shape, dim)


def mm(a, b):
    return jnp.dot(a, b, preferred_element_type=f32)


def attention_kernel(q_ref, k_ref, len_ref, up_ref, out_ref, lat_ref):
    def score_step(i, sums):
        rows = pl.ds(i * 16, 16)
        q = [q_ref[h, rows, :].astype(f32) for h in range(HEADS)]
        k = [k_ref[s, rows, :].astype(f32) for s in range(SLOTS)]
        new = []
        for h in range(HEADS):
            for s in range(SLOTS):
                prod = q[h] * k[s]
                new.append(sums[h * SLOTS + s] + (prod[:8] + prod[8:]))
        return tuple(new)

    sums = lax.fori_loop(
        0, WIDTH // 16, score_step, tuple(jnp.zeros((8, 128), f32) for _ in range(HEADS * SLOTS))
    )
    live = iota((SLOTS, 128), 0) < len_ref[...]
    probs = []
    for h in range(HEADS):
        scores = jnp.concatenate(
            [jnp.sum(sums[h * SLOTS + s], axis=0, keepdims=True) for s in range(SLOTS)], axis=0
        )
        scores = jnp.where(live, scores * score_scale, -1e30)
        expo = jnp.exp(scores - jnp.max(scores, axis=0, keepdims=True))
        prob = (expo / jnp.sum(expo, axis=0, keepdims=True)).astype(bf16).astype(f32)
        probs.append([jnp.broadcast_to(prob[s : s + 1], (8, 128)) for s in range(SLOTS)])

    @pl.loop(0, LATENT // 16)
    def _(i):
        rows = pl.ds(i * 16, 16)
        k = [k_ref[s, rows, :].astype(f32) for s in range(SLOTS)]
        for h in range(HEADS):
            low = sum(probs[h][s] * k[s][:8] for s in range(SLOTS))
            high = sum(probs[h][s] * k[s][8:] for s in range(SLOTS))
            lat_ref[h, rows, :] = jnp.concatenate([low, high], axis=0).astype(bf16)

    for h in range(HEADS):
        out_ref[:, h * VALUE : (h + 1) * VALUE] = lax.dot_general(
            lat_ref[h], up_ref[h], (((0,), (0,)), ((), ())), preferred_element_type=f32
        ).astype(bf16)


def attention(q, k, lengths, up):
    return pl.pallas_call(
        attention_kernel,
        grid=(REQUESTS // 128,),
        in_specs=[
            pl.BlockSpec((HEADS, WIDTH, 128), lambda j: (0, 0, j)),
            pl.BlockSpec((SLOTS, WIDTH, 128), lambda j: (0, 0, j)),
            pl.BlockSpec((1, 128), lambda j: (0, j)),
            pl.BlockSpec((HEADS, LATENT, VALUE), lambda j: (0, 0, 0)),
        ],
        out_specs=pl.BlockSpec((128, HEADS * VALUE), lambda j: (j, 0)),
        out_shape=jax.ShapeDtypeStruct((REQUESTS, HEADS * VALUE), bf16),
        scratch_shapes=[pltpu.VMEM((HEADS, LATENT, 128), bf16)],
        compiler_params=pltpu.CompilerParams(vmem_limit_bytes=VMEM_BYTES),
        cost_estimate=pl.CostEstimate(flops=40_000_000, bytes_accessed=4_200_000, transcendentals=8192),
        name="attention",
    )(q, k, lengths, up)


def plan_kernel(routes_ref, routes_t_ref, score_ref, place_ref, weight_ref):
    routes_t = routes_t_ref[...]
    named_t = jnp.zeros((EXPERTS, ROWS), f32)
    for k in range(TOP):
        named_t += (iota((EXPERTS, ROWS), 0) == routes_t[k : k + 1, :]).astype(f32)
    before_t = (iota((ROWS, ROWS), 0) < iota((ROWS, ROWS), 1)).astype(bf16)
    rank_t = mm(named_t.astype(bf16), before_t)
    spread = (iota((ROWS, 4 * ROWS), 1) % ROWS == iota((ROWS, 4 * ROWS), 0)).astype(bf16)
    expand = (iota((PIECES, EXPERTS), 0) // 8 == iota((PIECES, EXPERTS), 1)).astype(bf16)
    both = []
    for slot in range(2):
        here = jnp.where(rank_t == slot, named_t, 0.0).astype(bf16)
        both.append(mm(expand, mm(here, spread).astype(bf16)))
    n = iota((PIECES, 4 * ROWS), 0)
    place = jnp.where(n % 2 == 0, both[0], both[1])
    place_ref[...] = jnp.where(n % 8 // 2 == iota((PIECES, 4 * ROWS), 1) // ROWS, place, 0.0).astype(bf16)

    routes, scores = routes_ref[...], score_ref[...]
    gates = 2.5 * scores / jnp.sum(scores, axis=1, keepdims=True)
    named = jnp.zeros((ROWS, EXPERTS), f32)
    gate = jnp.zeros((ROWS, EXPERTS), f32)
    for k in range(TOP):
        hit = iota((ROWS, EXPERTS), 1) == routes[:, k : k + 1]
        named += hit.astype(f32)
        gate += jnp.where(hit, gates[:, k : k + 1], 0.0)
    before = (iota((ROWS, ROWS), 1) < iota((ROWS, ROWS), 0)).astype(bf16)
    rank = mm(before, named.astype(bf16))
    expand = (iota((EXPERTS, PIECES), 1) // 8 == iota((EXPERTS, PIECES), 0)).astype(bf16)
    n = iota((ROWS, PIECES), 1)
    high, low = [], []
    for slot in range(2):
        part = jnp.where(rank == slot, gate, 0.0)
        top = part.astype(bf16)
        high.append(mm(top, expand))
        low.append(mm((part - top.astype(f32)).astype(bf16), expand))
    for i, parts in enumerate((high, low)):
        row = jnp.where(n % 2 == 0, parts[0], parts[1])
        for quarter in range(4):
            weight_ref[pl.ds((i * 4 + quarter) * ROWS, ROWS), :] = jnp.where(
                n % 8 // 2 == quarter, row, 0.0
            ).astype(bf16)


def plan(routes, scores):
    return pl.pallas_call(
        plan_kernel,
        out_shape=(
            jax.ShapeDtypeStruct((PIECES, 4 * ROWS), bf16),
            jax.ShapeDtypeStruct((8 * ROWS, PIECES), bf16),
        ),
        compiler_params=pltpu.CompilerParams(vmem_limit_bytes=VMEM_BYTES),
        cost_estimate=pl.CostEstimate(flops=60_000_000, bytes_accessed=500_000, transcendentals=0),
        name="plan",
    )(routes, routes.T, scores)


def project_kernel(chip_ref, head_ref, *refs):
    blocks, out_ref, w_ref, sems = refs[:8], refs[8], refs[9], refs[10]
    z, core = chip_ref[0], chip_ref[1]

    def copy(i):
        chip = lax.rem(z + i // 2, 4)
        which = core if i % 2 == 0 else 1 - core
        start = pl.multiple_of((chip * 2 + which) * COLUMNS, 16)
        return pltpu.make_async_copy(blocks[i], w_ref.at[pl.ds(start, COLUMNS), :], sems.at[i])

    for i in range(8):
        copy(i).start()
    for step in range(4):
        copy(2 * step).wait()
        copy(2 * step + 1).wait()
        start = pl.multiple_of(lax.rem(z + step, 4) * QUARTER, 128)
        out_ref[:, pl.ds(start, QUARTER)] = lax.dot_general(
            head_ref[...],
            w_ref[pl.ds(start, QUARTER), :],
            (((1,), (1,)), ((), ())),
            preferred_element_type=f32,
        ).astype(bf16)


def project(chip, head_out, blocks):
    return pl.pallas_call(
        project_kernel,
        in_specs=[pl.BlockSpec(memory_space=pltpu.SMEM), pl.BlockSpec(memory_space=pltpu.VMEM)]
        + [pl.BlockSpec(memory_space=pl.ANY)] * 8,
        out_specs=pl.BlockSpec(memory_space=pltpu.VMEM),
        out_shape=jax.ShapeDtypeStruct((REQUESTS, D), bf16),
        scratch_shapes=[pltpu.VMEM((D, HEADS * VALUE), bf16), pltpu.SemaphoreType.DMA((8,))],
        compiler_params=pltpu.CompilerParams(vmem_limit_bytes=VMEM_BYTES),
        cost_estimate=pl.CostEstimate(flops=2 * REQUESTS * 512 * D, bytes_accessed=5_800_000, transcendentals=0),
        name="project",
    )(chip, head_out, *blocks)


def dispatch_kernel(parts_ref, res_ref, gain_ref, place_ref, hidden_ref, out_ref, norm_ref):
    total = parts_ref[0].astype(f32)
    for i in range(1, parts_ref.shape[0]):
        total += parts_ref[i].astype(f32)
    hidden = (res_ref[...].astype(f32) + total.astype(bf16).astype(f32)).astype(bf16)
    hidden_ref[...] = hidden
    hidden = hidden.astype(f32)
    inverse = lax.rsqrt(jnp.mean(hidden * hidden, axis=1, keepdims=True) + 1e-6)
    normed = (hidden * inverse * gain_ref[...]).astype(bf16)
    for quarter in range(4):
        norm_ref[pl.ds(quarter * ROWS, ROWS), :] = normed[:, quarter * QUARTER : (quarter + 1) * QUARTER]

    @pl.loop(0, 4)
    def _(i):
        rows = pl.ds(i * (PIECES // 4), PIECES // 4)
        out_ref[rows, :] = mm(place_ref[rows, :], norm_ref[...]).astype(bf16)


def dispatch(parts, residual, gain, place):
    return pl.pallas_call(
        dispatch_kernel,
        out_shape=(
            jax.ShapeDtypeStruct((ROWS, D), bf16),
            jax.ShapeDtypeStruct((PIECES, QUARTER), bf16),
        ),
        scratch_shapes=[pltpu.VMEM((4 * ROWS, QUARTER), bf16)],
        compiler_params=pltpu.CompilerParams(vmem_limit_bytes=VMEM_BYTES),
        cost_estimate=pl.CostEstimate(flops=120_000_000, bytes_accessed=4_000_000, transcendentals=16),
        name="dispatch",
    )(parts, residual, gain, place)


def expert_kernel(x_ref, wi_ref, wo_ref, out_ref, rows_ref, act_ref, back_ref, wi_buf, wo_buf, sems):
    half = FF // 4

    def copy_in(i):
        return pltpu.make_async_copy(
            wi_ref.at[:, pl.ds((i % 2) * FF + (i // 2) * half, half)], wi_buf.at[i], sems.at[i]
        )

    def copy_out(i):
        return pltpu.make_async_copy(
            wo_ref.at[:, pl.ds(i * QUARTER, QUARTER)], wo_buf.at[i], sems.at[8 + i]
        )

    for i in range(8):
        copy_in(i).start()
    for i in range(4):
        copy_out(i).start()

    def matches(to, frm):
        same_quarter = to // 64 == frm % 8 // 2
        return (same_quarter & (to % 64 // 2 == frm // 8) & (to % 2 == frm % 2)).astype(bf16)

    sort = matches(iota((256, 256), 0), iota((256, 256), 1))
    unsort = matches(iota((256, 256), 1), iota((256, 256), 0))
    for b in range(4):
        sorted_rows = mm(sort, x_ref[b * 256 : (b + 1) * 256, :]).astype(bf16)
        for quarter in range(4):
            rows_ref[b * 64 : (b + 1) * 64, quarter * QUARTER : (quarter + 1) * QUARTER] = sorted_rows[
                quarter * 64 : (quarter + 1) * 64
            ]

    for i in range(4):
        copy_in(2 * i).wait()
        copy_in(2 * i + 1).wait()
        gate = mm(rows_ref[...], wi_buf[2 * i])
        up = mm(rows_ref[...], wi_buf[2 * i + 1])
        act_ref[:, i * half : (i + 1) * half] = (jax.nn.silu(gate) * up).astype(bf16)

    for quarter in range(4):
        copy_out(quarter).wait()
        result = mm(act_ref[...], wo_buf[quarter]).astype(bf16)
        for b in range(4):
            back_ref[b, quarter * 64 : (quarter + 1) * 64, :] = result[b * 64 : (b + 1) * 64]
    for b in range(4):
        out_ref[b * 256 : (b + 1) * 256, :] = mm(unsort, back_ref[b]).astype(bf16)


def expert(pieces, w_in, w_out):
    rows = 2 * EXPERTS
    return pl.pallas_call(
        expert_kernel,
        in_specs=[
            pl.BlockSpec(memory_space=pltpu.VMEM),
            pl.BlockSpec(memory_space=pl.ANY),
            pl.BlockSpec(memory_space=pl.ANY),
        ],
        out_specs=pl.BlockSpec(memory_space=pltpu.VMEM),
        out_shape=jax.ShapeDtypeStruct((PIECES, QUARTER), bf16),
        scratch_shapes=[
            pltpu.VMEM((rows, D), bf16),
            pltpu.VMEM((rows, FF), bf16),
            pltpu.VMEM((4, 256, QUARTER), bf16),
            pltpu.VMEM((8, D, FF // 4), bf16),
            pltpu.VMEM((4, FF, QUARTER), bf16),
            pltpu.SemaphoreType.DMA((12,)),
        ],
        compiler_params=pltpu.CompilerParams(vmem_limit_bytes=VMEM_BYTES),
        cost_estimate=pl.CostEstimate(
            flops=2 * rows * 3 * D * FF, bytes_accessed=26_000_000, transcendentals=rows * FF
        ),
        name="expert",
    )(pieces, w_in, w_out)


def combine_kernel(back_ref, weight_ref, hidden_ref, out_ref):
    both = mm(weight_ref[...], back_ref[...])
    for quarter in range(4):
        columns = slice(quarter * QUARTER, (quarter + 1) * QUARTER)
        rows = slice(quarter * ROWS, (quarter + 1) * ROWS)
        low_rows = slice((4 + quarter) * ROWS, (5 + quarter) * ROWS)
        out_ref[:, columns] = (hidden_ref[:, columns].astype(f32) + (both[rows] + both[low_rows])).astype(bf16)


def combine(back, weight, hidden):
    return pl.pallas_call(
        combine_kernel,
        out_shape=jax.ShapeDtypeStruct((ROWS, D), bf16),
        compiler_params=pltpu.CompilerParams(vmem_limit_bytes=VMEM_BYTES),
        cost_estimate=pl.CostEstimate(flops=240_000_000, bytes_accessed=2_400_000, transcendentals=0),
        name="combine",
    )(back, weight, hidden)


def local(
    queries,
    cached_latent_rows,
    lengths,
    value_up_weight,
    out_proj,
    residual_in,
    norm_gain,
    routes,
    route_scores,
    w_gate_up,
    w_down,
):
    own = out_proj.T
    blocks = [own] + [
        lax.ppermute(own, "z", [(i, (i - step) % 4) for i in range(4)]) for step in (1, 2, 3)
    ]
    pairs = []
    for block in blocks:
        pairs += [block, lax.ppermute(block, "core", [(0, 1), (1, 0)])]
    chip = jnp.stack([lax.axis_index("z"), lax.axis_index("core")]).astype(jnp.int32)

    head_out = attention(
        queries.transpose(1, 2, 0),
        cached_latent_rows.transpose(1, 2, 0),
        lengths.reshape(1, REQUESTS),
        value_up_weight,
    )
    place, weight = plan(routes, route_scores)
    shares = project(chip, head_out, pairs)
    parts = lax.all_to_all(
        shares.reshape(16, ROWS, D), ("y", "x"), split_axis=0, concat_axis=0, tiled=True
    )
    hidden, outgoing = dispatch(parts, residual_in, norm_gain.reshape(1, D), place)
    everyone = ("z", "core", "y", "x")
    arrived = lax.all_to_all(
        outgoing.reshape(EXPERTS, 8, QUARTER), everyone, split_axis=0, concat_axis=0, tiled=True
    )
    produced = expert(arrived.reshape(PIECES, QUARTER), w_gate_up[0], w_down[0])
    returned = lax.all_to_all(
        produced.reshape(EXPERTS, 8, QUARTER), everyone, split_axis=0, concat_axis=0, tiled=True
    )
    return combine(returned.reshape(PIECES, QUARTER), weight, hidden)


def solution(mesh):
    fine = Mesh(mesh.devices.reshape(4, 2, 4, 4), ("z", "core", "y", "x"))
    dp, ex, both = ("z", "core"), ("y", "x"), ("z", "core", "y", "x")
    in_specs = (
        P(dp, ex, None),
        P(dp, None, None),
        P(dp),
        P(ex, None, None),
        P(ex, dp),
        P(both, None),
        P(),
        P(both, None),
        P(both, None),
        P(both, None, None),
        P(both, None, None),
    )
    return jax.shard_map(local, mesh=fine, in_specs=in_specs, out_specs=P(both, None), check_vma=False)
```

time: 225 us -> 167 us (0.74)
  waiting for transfers between devices: 112 us -> 44 us
  Pallas kernels: 0 us -> 35 us
  matrix products: 31.5 us -> 0 us
  blocking collectives: 36 us -> 65.4 us
  local copies, waits for them, and re-layouts: 23.2 us -> 4.98 us
  between operations: 13.6 us -> 0.12 us
  starting transfers between devices: 4.84 us -> 16.3 us
  other arithmetic: 3.96 us -> 0.66 us
    reduce_scatter x1 -> x0, waiting for transfers between devices: 71.2 us -> none  [local(): lax.psum_scatter(jnp.dot(flat_heads, full_proj, preferred_element_type=jn...]
    pallas_call x0 -> x6, Pallas kernels: none -> 35 us  [the longest x1 12.9 us: expert(): pl.pallas_call(expert_kernel, in_specs=[pl.BlockSpec(memory_space=pltpu.V...]
    dot_general x8 -> x0, matrix products: 31.5 us -> none  [the longest x1 7.26 us: local(): both = jnp.dot(flat_in, w_gate_up[0], preferred_element_type=jnp.float32)]
    all_to_all x1 -> x2, blocking collectives: 36 us -> 65.4 us  [the longest x1 32.7 us: local(): lax.all_to_all(outgoing.reshape(EXPERTS, 8, QUARTER), everyone, split_axi...]
    ppermute x0 -> x7, waiting for transfers between devices: none -> 19.4 us  [the longest x3 19.4 us: local(): lax.ppermute(own, 'z', [(i, (i - step) % 4) for i in range(4)])]
    all_gather x1 -> x0, waiting for transfers between devices: 12.8 us -> none  [local(): full_proj = lax.all_gather(out_proj, 'dp', axis=1, tiled=True)]
    reshape x4 -> x1, local copies, waits for them, and re-layouts: 11.3 us -> 0.61 us  [local(): norm_gain.reshape(1, D)]
    ppermute x0 -> x7, starting transfers between devices: none -> 9.41 us  [the longest x3 5.29 us: local(): lax.ppermute(own, 'z', [(i, (i - step) % 4) for i in range(4)])]
  transfers between devices with their start and end apart: 3 -> 8, of which waited for: 3 -> 3; matrix products, arithmetic and copies ran while one was open for 10% -> 2% of each run, Pallas kernels for 0% -> 6%
where the time goes in v1:
time: 167 us; the launch traced here: 166 us
  blocking collectives  65.4 us (39%)
  waiting for transfers between devices  44 us (26%)
  Pallas kernels  35 us (21%)
  starting transfers between devices  16.3 us (10%)
  local copies, waits for them, and re-layouts  4.98 us (3%)
    all_to_all x1, blocking collectives, local(): lax.all_to_all(outgoing.reshape(EXPERTS, 8, QUARTER), everyone, split_axi...  32.7 us
    all_to_all x1, blocking collectives, local(): lax.all_to_all(produced.reshape(EXPERTS, 8, QUARTER), everyone, split_axi...  32.7 us
    all_to_all x1, waiting for transfers between devices, local(): lax.all_to_all(shares.reshape(16, ROWS, D), ('y', 'x'), split_axis=0, con...  24.6 us
    ppermute x3, waiting for transfers between devices, local(): lax.ppermute(own, 'z', [(i, (i - step) % 4) for i in range(4)])  19.4 us
    pallas_call x1, Pallas kernels, expert(): pl.pallas_call(expert_kernel, in_specs=[pl.BlockSpec(memory_space=pltpu.V...  12.9 us
    pallas_call x1, Pallas kernels, attention(): pl.pallas_call(attention_kernel, grid=(REQUESTS // 128,), in_specs=[pl.Bl...  7.48 us
    all_to_all x1, starting transfers between devices, local(): lax.all_to_all(shares.reshape(16, ROWS, D), ('y', 'x'), split_axis=0, con...  6.9 us
    pallas_call x1, Pallas kernels, project(): pl.pallas_call(project_kernel, in_specs=[pl.BlockSpec(memory_space=pltpu....  5.35 us
  transfers between devices with their start and end apart: 8, of which 3 were waited for; matrix products, arithmetic and copies ran while one was open for 2% of the time, Pallas kernels for 6%

profile of v1, /device:TPU:1, one launch (start us, length us, event | category | flops | bytes accessed | tf_op | source)
XLA Modules:
  0.0 166.5 jit_solution(13979837274060400980)
XLA Ops:
  0.0 4.6 %collective-permute-start.1 = (bf16[448,512]{1,0:T(8,128)(2,1)}, bf16[448,512]{1,0:T(8,128)(2,1)S(1)}, u32[]{:S(2)}, u32[]{:S(2)}) collective-permute-start(bf16[448,512]{1,0:T(8,128)(2,1)} %bitcast.23), channel_id=1, source_target_pairs={{0,96},{32,0},{64,32},{96,64},{1,97},{33,1},{65,33},{97,65},{2,98}... | collective-permute-start | bytes 1376264 | tf_op jit(solution)/shard_map/ppermute | solution.py:333
  4.6 0.7 collective-permute-start.5
  5.3 1.5 collective-permute-start
  6.8 17.0 %collective-permute-done.1.refs_2_ = bf16[448,512]{1,0:T(8,128)(2,1)S(1)} collective-permute-done((bf16[448,512]{1,0:T(8,128)(2,1)}, bf16[448,512]{1,0:T(8,128)(2,1)S(1)}, u32[]{:S(2)}, u32[]{:S(2)}) %collective-permute-start.1) | collective-permute-done | bytes 458784 | tf_op jit(solution)/shard_map/ppermute | solution.py:333
  23.8 1.7 %collective-permute-start.2 = (bf16[448,512]{1,0:T(8,128)(2,1)S(1)}, bf16[448,512]{1,0:T(8,128)(2,1)S(1)}, u32[]{:S(2)}, u32[]{:S(2)}) collective-permute-start(bf16[448,512]{1,0:T(8,128)(2,1)S(1)} %collective-permute-done.1.refs_2_), channel_id=1, source_target_pairs={{0,16},{16,0},{1,17},{17,1},{2,18},{18,2},{3,19},{19,3},{4,20},{20... | collective-permute-start | bytes 1376264 | tf_op jit(solution)/shard_map/ppermute | solution.py:337
  25.6 2.4 %collective-permute-done.5.refs_6_ = bf16[448,512]{1,0:T(8,128)(2,1)S(1)} collective-permute-done((bf16[448,512]{1,0:T(8,128)(2,1)}, bf16[448,512]{1,0:T(8,128)(2,1)S(1)}, u32[]{:S(2)}, u32[]{:S(2)}) %collective-permute-start.5) | collective-permute-done | bytes 458784 | tf_op jit(solution)/shard_map/ppermute | solution.py:333
  27.9 0.8 collective-permute-start.6
  28.8 7.5 %attention.1.head_ref = bf16[256,512]{1,0:T(8,128)(2,1)} custom-call(bf16[4,576,256]{2,1,0:T(8,128)(2,1)} %bitcast.22, bf16[8,576,256]{2,1,0:T(8,128)(2,1)} %bitcast.20, s32[1,256]{1,0:T(1,128)} %bitcast.29, bf16[4,512,128]{2,1,0:T(8,128)(2,1)} %up_ref.1), custom_call_target="tpu_custom_call" | custom-call | flops 40000000 | bytes 4200000 | tf_op jit(solution)/shard_map/attention/pallas_call | solution.py:81
  36.3 0.7 pad_add_fusion.chip_ref
  37.0 0.7 copy-done.4
  38.0 0.8 copy-done.7
  38.8 5.3 %project.1 = bf16[256,3584]{1,0:T(8,128)(2,1)} custom-call(s32[2]{0:T(128)} %pad_add_fusion.chip_ref, bf16[256,512]{1,0:T(8,128)(2,1)} %attention.1.head_ref, bf16[448,512]{1,0:T(8,128)(2,1)} %bitcast.27, bf16[448,512]{1,0:T(8,128)(2,1)} %copy-done.4, bf16[448,512]{1,0:T(8,128)(2,1)} %copy-done.1, bf16[448,512]{1,0:T(8,128)(2,1)} %copy-done.5, ...), custom_call_target="tpu_custom_call" | custom-call | flops 939524096 | bytes 5800000 | tf_op jit(solution)/shard_map/project/pallas_call | solution.py:180
  44.2 6.9 %all-to-all-start = ((bf16[16,16,3584]{2,1,0:T(8,128)(2,1)}), bf16[16,16,3584]{2,1,0:T(8,128)(2,1)S(1)}, u32[]{:S(2)}, u32[]{:S(2)}) async-start(bf16[16,16,3584]{2,1,0:T(8,128)(2,1)} %bitcast.18), calls=%async_computation | async-start | bytes 3670016 | tf_op jit(solution)/shard_map/all_to_all | solution.py:348
  51.1 0.7 copy.12.routes_ref
  51.8 0.7 copy.13.score_ref
  52.4 0.6 reshape.23.gain_ref
  53.0 2.3 %plan.1 = (bf16[1024,64]{1,0:T(8,128)(2,1)}, bf16[128,1024]{1,0:T(8,128)(2,1)}) custom-call(s32[16,8]{1,0:T(8,128)} %copy.12.routes_ref, s32[8,16]{1,0:T(8,128)} %bitcast.28, f32[16,8]{1,0:T(8,128)} %copy.13.score_ref), custom_call_target="tpu_custom_call" | custom-call | flops 60000000 | bytes 500000 | tf_op jit(solution)/shard_map/plan/pallas_call | solution.py:143
  55.3 24.6 %all-to-all-done.parts_ref = bf16[16,16,3584]{2,1,0:T(8,128)(2,1)S(1)} async-done(((bf16[16,16,3584]{2,1,0:T(8,128)(2,1)}), bf16[16,16,3584]{2,1,0:T(8,128)(2,1)S(1)}, u32[]{:S(2)}, u32[]{:S(2)}) %all-to-all-start) | async-done | bytes 1835040 | tf_op jit(solution)/shard_map/all_to_all | solution.py:348
  79.9 1.2 copy-done
  81.2 4.4 %dispatch.1 = (bf16[16,3584]{1,0:T(8,128)(2,1)}, bf16[1024,896]{1,0:T(8,128)(2,1)}) custom-call(bf16[16,16,3584]{2,1,0:T(8,128)(2,1)} %copy-done, bf16[16,3584]{1,0:T(8,128)(2,1)} %res_ref.1, f32[1,3584]{1,0:T(1,128)} %reshape.23.gain_ref, bf16[1024,64]{1,0:T(8,128)(2,1)} %get-tuple-element.9.place_ref), custom_call_target="tpu_custom_call" | custom-call | flops 120000000 | bytes 4000000 | tf_op jit(solution)/shard_map/dispatch/pallas_call | solution.py:212
  85.5 32.7 %all_to_all.15 = bf16[128,8,896]{2,1,0:T(8,128)(2,1)} all-to-all(bf16[128,8,896]{2,1,0:T(8,128)(2,1)} %bitcast.21), channel_id=1, replica_groups=mesh['z'=4,'core'=2,'y'=4,'x'=4] {'z','core','y','x'}, dimensions={0} | all-to-all | bytes 3670016 | tf_op jit(solution)/shard_map/all_to_all | solution.py:353
  118.3 12.9 %expert.1 = bf16[1024,896]{1,0:T(8,128)(2,1)} custom-call(bf16[1024,896]{1,0:T(8,128)(2,1)} %bitcast.15, bf16[3584,2048]{1,0:T(8,128)(2,1)} %bitcast.14, bf16[1024,3584]{1,0:T(8,128)(2,1)} %bitcast.19), custom_call_target="tpu_custom_call" | custom-call | flops 5637144576 | bytes 26000000 | tf_op jit(solution)/shard_map/expert/pallas_call | solution.py:274
  131.1 32.7 %all_to_all.16 = bf16[128,8,896]{2,1,0:T(8,128)(2,1)} all-to-all(bf16[128,8,896]{2,1,0:T(8,128)(2,1)} %bitcast.16), channel_id=1, replica_groups=mesh['z'=4,'core'=2,'y'=4,'x'=4] {'z','core','y','x'}, dimensions={0} | all-to-all | bytes 3670016 | tf_op jit(solution)/shard_map/all_to_all | solution.py:357
  163.8 2.7 %combine.1 = bf16[16,3584]{1,0:T(8,128)(2,1)} custom-call(bf16[1024,896]{1,0:T(8,128)(2,1)} %bitcast.17, bf16[128,1024]{1,0:T(8,128)(2,1)} %get-tuple-element.11.weight_ref, bf16[16,3584]{1,0:T(8,128)(2,1)} %get-tuple-element.12.hidden_ref), custom_call_target="tpu_custom_call" | custom-call | flops 240000000 | bytes 2400000 | tf_op jit(solution)/shard_map/combine/pallas_call | solution.py:309
  (26 shorter events, 0.5 us)
Async XLA Ops:
  0.0 23.8 %collective-permute-start.1 = (bf16[448,512]{1,0:T(8,128)(2,1)}, bf16[448,512]{1,0:T(8,128)(2,1)S(1)}, u32[]{:S(2)}, u32[]{:S(2)}) collective-permute-start(bf16[448,512]{1,0:T(8,128)(2,1)} %bitcast.23), channel_id=1, source_target_pairs={{0,96},{32,0},{64,32},{96,64},{1,97},{33,1},{65,33},{97,65},{2,98}... | collective-permute-start | bytes 1376264 | tf_op jit(solution)/shard_map/ppermute | solution.py:333
  4.6 20.9 %collective-permute-start.3 = (bf16[448,512]{1,0:T(8,128)(2,1)}, bf16[448,512]{1,0:T(8,128)(2,1)S(1)}, u32[]{:S(2)}, u32[]{:S(2)}) collective-permute-start(bf16[448,512]{1,0:T(8,128)(2,1)} %bitcast.24), channel_id=1, source_target_pairs={{0,64},{32,96},{64,0},{96,32},{1,65},{33,97},{65,1},{97,33},{2,66}... | collective-permute-start | bytes 1376264 | tf_op jit(solution)/shard_map/ppermute | solution.py:333
  4.6 23.3 %collective-permute-start.5 = (bf16[448,512]{1,0:T(8,128)(2,1)}, bf16[448,512]{1,0:T(8,128)(2,1)S(1)}, u32[]{:S(2)}, u32[]{:S(2)}) collective-permute-start(bf16[448,512]{1,0:T(8,128)(2,1)} %bitcast.25), channel_id=1, source_target_pairs={{0,32},{32,64},{64,96},{96,0},{1,33},{33,65},{65,97},{97,1},{2,34}... | collective-permute-start | bytes 1376264 | tf_op jit(solution)/shard_map/ppermute | solution.py:333
  5.3 31.7 %collective-permute-start = (bf16[448,512]{1,0:T(8,128)(2,1)}, bf16[448,512]{1,0:T(8,128)(2,1)S(1)}, u32[]{:S(2)}, u32[]{:S(2)}) collective-permute-start(bf16[448,512]{1,0:T(8,128)(2,1)} %bitcast.26), channel_id=1, source_target_pairs={{0,16},{16,0},{1,17},{17,1},{2,18},{18,2},{3,19},{19,3},{4,20},{20... | collective-permute-start | bytes 1376264 | tf_op jit(solution)/shard_map/ppermute | solution.py:337
  23.8 12.5 %copy-start.1 = (bf16[448,512]{1,0:T(8,128)(2,1)}, bf16[448,512]{1,0:T(8,128)(2,1)S(1)}, u32[]{:S(2)}) copy-start(bf16[448,512]{1,0:T(8,128)(2,1)S(1)} %collective-permute-done.1.refs_2_) | copy-start | bytes 1376260
  23.8 13.2 %collective-permute-start.2 = (bf16[448,512]{1,0:T(8,128)(2,1)S(1)}, bf16[448,512]{1,0:T(8,128)(2,1)S(1)}, u32[]{:S(2)}, u32[]{:S(2)}) collective-permute-start(bf16[448,512]{1,0:T(8,128)(2,1)S(1)} %collective-permute-done.1.refs_2_), channel_id=1, source_target_pairs={{0,16},{16,0},{1,17},{17,1},{2,18},{18,2},{3,19},{19,3},{4,20},{20... | collective-permute-start | bytes 1376264 | tf_op jit(solution)/shard_map/ppermute | solution.py:337
  25.5 10.8 %copy-start.2 = (bf16[448,512]{1,0:T(8,128)(2,1)}, bf16[448,512]{1,0:T(8,128)(2,1)S(1)}, u32[]{:S(2)}) copy-start(bf16[448,512]{1,0:T(8,128)(2,1)S(1)} %collective-permute-done.3.refs_4_) | copy-start | bytes 1376260
  25.5 11.5 %collective-permute-start.4 = (bf16[448,512]{1,0:T(8,128)(2,1)S(1)}, bf16[448,512]{1,0:T(8,128)(2,1)S(1)}, u32[]{:S(2)}, u32[]{:S(2)}) collective-permute-start(bf16[448,512]{1,0:T(8,128)(2,1)S(1)} %collective-permute-done.3.refs_4_), channel_id=1, source_target_pairs={{0,16},{16,0},{1,17},{17,1},{2,18},{18,2},{3,19},{19,3},{4,20},{20... | collective-permute-start | bytes 1376264 | tf_op jit(solution)/shard_map/ppermute | solution.py:337
  27.9 8.3 %copy-start.3 = (bf16[448,512]{1,0:T(8,128)(2,1)}, bf16[448,512]{1,0:T(8,128)(2,1)S(1)}, u32[]{:S(2)}) copy-start(bf16[448,512]{1,0:T(8,128)(2,1)S(1)} %collective-permute-done.5.refs_6_) | copy-start | bytes 1376260
  27.9 9.0 %collective-permute-start.6 = (bf16[448,512]{1,0:T(8,128)(2,1)S(1)}, bf16[448,512]{1,0:T(8,128)(2,1)S(1)}, u32[]{:S(2)}, u32[]{:S(2)}) collective-permute-start(bf16[448,512]{1,0:T(8,128)(2,1)S(1)} %collective-permute-done.5.refs_6_), channel_id=1, source_target_pairs={{0,16},{16,0},{1,17},{17,1},{2,18},{18,2},{3,19},{19,3},{4,20},{20... | collective-permute-start | bytes 1376264 | tf_op jit(solution)/shard_map/ppermute | solution.py:337
  36.9 0.8 copy-start.4
  37.0 0.9 copy-start.5
  37.0 1.1 copy-start.6
  38.0 0.8 copy-start.7
  44.1 6.9 %copy-start.10 = (s32[16,8]{0,1:T(8,128)S(1)}, s32[16,8]{0,1:T(8,128)}, u32[]{:S(2)}) copy-start(s32[16,8]{0,1:T(8,128)} %param.18) | copy-start | bytes 1540
  44.2 7.6 %copy-start.9 = (f32[16,8]{0,1:T(8,128)S(1)}, f32[16,8]{0,1:T(8,128)}, u32[]{:S(2)}) copy-start(f32[16,8]{0,1:T(8,128)} %param.19) | copy-start | bytes 1540
  44.2 8.3 %copy-start.8 = (f32[3584]{0:T(1024)S(1)}, f32[3584]{0:T(1024)}, u32[]{:S(2)}) copy-start(f32[3584]{0:T(1024)} %param.17) | copy-start | bytes 43012
  44.2 35.8 %all-to-all-start = ((bf16[16,16,3584]{2,1,0:T(8,128)(2,1)}), bf16[16,16,3584]{2,1,0:T(8,128)(2,1)S(1)}, u32[]{:S(2)}, u32[]{:S(2)}) async-start(bf16[16,16,3584]{2,1,0:T(8,128)(2,1)} %bitcast.18), calls=%async_computation | async-start | bytes 3670016 | tf_op jit(solution)/shard_map/all_to_all | solution.py:348
  79.9 1.2 copy-start

commit v2 on v1

--- a/solution.py
+++ b/solution.py
@@ -21,11 +21,12 @@
 QUARTER = D // 4
 PIECES = EXPERTS * 8
 COLUMNS = 448
+STEPS, DEPTH = 7, D // 7
 
 score_scale = 0.07216878364870323
 
 f32, bf16 = jnp.float32, jnp.bfloat16
-VMEM_BYTES = 56 * 1024 * 1024
+VMEM_BYTES = 16 * 1024 * 1024
 
 
 def iota(shape, dim):
@@ -91,7 +92,7 @@
         out_shape=jax.ShapeDtypeStruct((REQUESTS, HEADS * VALUE), bf16),
         scratch_shapes=[pltpu.VMEM((HEADS, LATENT, 128), bf16)],
         compiler_params=pltpu.CompilerParams(vmem_limit_bytes=VMEM_BYTES),
-        cost_estimate=pl.CostEstimate(flops=40_000_000, bytes_accessed=4_200_000, transcendentals=8192),
+        cost_estimate=pl.CostEstimate(flops=9_000_000_000, bytes_accessed=4_200_000, transcendentals=8192),
         name="attention",
     )(q, k, lengths, up)
 
@@ -152,49 +153,125 @@
     )(routes, routes.T, scores)
 
 
-def project_kernel(chip_ref, head_ref, *refs):
-    blocks, out_ref, w_ref, sems = refs[:8], refs[8], refs[9], refs[10]
-    z, core = chip_ref[0], chip_ref[1]
-
-    def copy(i):
-        chip = lax.rem(z + i // 2, 4)
-        which = core if i % 2 == 0 else 1 - core
-        start = pl.multiple_of((chip * 2 + which) * COLUMNS, 16)
-        return pltpu.make_async_copy(blocks[i], w_ref.at[pl.ds(start, COLUMNS), :], sems.at[i])
-
-    for i in range(8):
-        copy(i).start()
+def hold_kernel(next_ref, last_ref, after_ref, next_out, last_out):
+    next_out[...] = next_ref[...]
+    last_out[...] = last_ref[...]
+
+
+def hold(next_block, last_block, after):
+    block = jax.ShapeDtypeStruct((COLUMNS, HEADS * VALUE), bf16)
+    whole = pl.BlockSpec((COLUMNS, HEADS * VALUE), lambda i: (0, 0))
+    return pl.pallas_call(
+        hold_kernel,
+        grid=(1,),
+        in_specs=[whole, whole, pl.BlockSpec((16, 128), lambda i: (0, 0))],
+        out_specs=[whole, whole],
+        out_shape=[block, block],
+        compiler_params=pltpu.CompilerParams(vmem_limit_bytes=VMEM_BYTES),
+        cost_estimate=pl.CostEstimate(flops=0, bytes_accessed=2_000_000, transcendentals=0),
+        name="hold",
+    )(next_block, last_block, after)
+
+
+def project_kernel(first, chips, at_ref, head_ref, *refs):
+    blocks, outs, (rows_ref, w_ref) = refs[: 2 * chips], refs[2 * chips : 2 * chips + 4], refs[2 * chips + 4 :]
+    y, x, core = at_ref[1], at_ref[2], at_ref[3]
     for step in range(4):
-        copy(2 * step).wait()
-        copy(2 * step + 1).wait()
+        for other in range(4):
+            if first == "x":
+                start = other * 64 + lax.rem(x + step, 4) * ROWS
+            else:
+                start = lax.rem(y + step, 4) * 64 + other * ROWS
+            rows_ref[pl.ds(step * 64 + other * ROWS, ROWS), :] = head_ref[
+                pl.ds(pl.multiple_of(start, ROWS), ROWS), :
+            ]
+    for i in range(chips):
+        own = pl.multiple_of(core * COLUMNS, 16)
+        other = pl.multiple_of((1 - core) * COLUMNS, 16)
+        w_ref[i, pl.ds(own, COLUMNS), :] = blocks[2 * i][...]
+        w_ref[i, pl.ds(other, COLUMNS), :] = blocks[2 * i + 1][...]
+        result = lax.dot_general(
+            rows_ref[...], w_ref[i], (((1,), (1,)), ((), ())), preferred_element_type=f32
+        ).astype(bf16)
+        for step in range(4):
+            outs[step][:, i * QUARTER : (i + 1) * QUARTER] = result[step * 64 : (step + 1) * 64]
+
+
+def project(first, at, head_out, blocks):
+    chips = len(blocks) // 2
+    return pl.pallas_call(
+        functools.partial(project_kernel, first, chips),
+        in_specs=[pl.BlockSpec(memory_space=pltpu.SMEM)]
+        + [pl.BlockSpec(memory_space=pltpu.VMEM)] * (1 + 2 * chips),
+        out_shape=[jax.ShapeDtypeStruct((64, chips * QUARTER), bf16)] * 4,
+        scratch_shapes=[
+            pltpu.VMEM((REQUESTS, HEADS * VALUE), bf16),
+            pltpu.VMEM((chips, QUARTER, HEADS * VALUE), bf16),
+        ],
+        compiler_params=pltpu.CompilerParams(vmem_limit_bytes=VMEM_BYTES),
+        cost_estimate=pl.CostEstimate(
+            flops=chips * REQUESTS * 512 * QUARTER * 2, bytes_accessed=chips * 1_500_000, transcendentals=0
+        ),
+        name="project_" + first,
+    )(at, head_out, *blocks)
+
+
+def reduce_kernel(second, place_ref, *refs):
+    parts, outs = refs[:4], refs[4:]
+    me = place_ref[1] if second == "y" else place_ref[2]
+    for step in range(4):
+        rows = pl.ds(pl.multiple_of(lax.rem(me + step, 4) * ROWS, ROWS), ROWS)
+        total = parts[0][rows, :].astype(f32)
+        for part in parts[1:]:
+            total += part[rows, :].astype(f32)
+        outs[step][...] = total.astype(bf16)
+
+
+def reduce(second, place, parts):
+    return pl.pallas_call(
+        functools.partial(reduce_kernel, second),
+        in_specs=[pl.BlockSpec(memory_space=pltpu.SMEM)] + [pl.BlockSpec(memory_space=pltpu.VMEM)] * 4,
+        out_shape=[jax.ShapeDtypeStruct((ROWS, parts[0].shape[1]), bf16)] * 4,
+        compiler_params=pltpu.CompilerParams(vmem_limit_bytes=VMEM_BYTES),
+        cost_estimate=pl.CostEstimate(flops=500_000, bytes_accessed=1_200_000, transcendentals=0),
+        name="reduce_" + second,
+    )(place, *parts)
+
+
+def total_kernel(*refs):
+    total = refs[0][...].astype(f32)
+    for part in refs[1:4]:
+        total += part[...].astype(f32)
+    refs[4][...] = total.astype(bf16)
+
+
+def total(parts):
+    return pl.pallas_call(
+        total_kernel,
+        out_shape=jax.ShapeDtypeStruct(parts[0].shape, bf16),
+        compiler_params=pltpu.CompilerParams(vmem_limit_bytes=VMEM_BYTES),
+        cost_estimate=pl.CostEstimate(flops=100_000, bytes_accessed=200_000, transcendentals=0),
+        name="total",
+    )(*parts)
+
+
+def exchange(axis, parts):
+    return [parts[0]] + [
+        lax.ppermute(parts[step], axis, [(i, (i + step) % 4) for i in range(4)]) for step in (1, 2, 3)
+    ]
+
+
+def dispatch_kernel(at_ref, *refs):
+    parts, (res_ref, gain_ref, place_ref, hidden_ref, out_ref, norm_ref, sum_ref) = refs[:5], refs[5:]
+    z = at_ref[0]
+    near = parts[0][...].astype(f32)
+    for part in parts[1:4]:
+        near += part[...].astype(f32)
+    far = parts[4][...].astype(f32)
+    for i, step in enumerate((0, 1, 3, 2)):
         start = pl.multiple_of(lax.rem(z + step, 4) * QUARTER, 128)
-        out_ref[:, pl.ds(start, QUARTER)] = lax.dot_general(
-            head_ref[...],
-            w_ref[pl.ds(start, QUARTER), :],
-            (((1,), (1,)), ((), ())),
-            preferred_element_type=f32,
-        ).astype(bf16)
-
-
-def project(chip, head_out, blocks):
-    return pl.pallas_call(
-        project_kernel,
-        in_specs=[pl.BlockSpec(memory_space=pltpu.SMEM), pl.BlockSpec(memory_space=pltpu.VMEM)]
-        + [pl.BlockSpec(memory_space=pl.ANY)] * 8,
-        out_specs=pl.BlockSpec(memory_space=pltpu.VMEM),
-        out_shape=jax.ShapeDtypeStruct((REQUESTS, D), bf16),
-        scratch_shapes=[pltpu.VMEM((D, HEADS * VALUE), bf16), pltpu.SemaphoreType.DMA((8,))],
-        compiler_params=pltpu.CompilerParams(vmem_limit_bytes=VMEM_BYTES),
-        cost_estimate=pl.CostEstimate(flops=2 * REQUESTS * 512 * D, bytes_accessed=5_800_000, transcendentals=0),
-        name="project",
-    )(chip, head_out, *blocks)
-
-
-def dispatch_kernel(parts_ref, res_ref, gain_ref, place_ref, hidden_ref, out_ref, norm_ref):
-    total = parts_ref[0].astype(f32)
-    for i in range(1, parts_ref.shape[0]):
-        total += parts_ref[i].astype(f32)
-    hidden = (res_ref[...].astype(f32) + total.astype(bf16).astype(f32)).astype(bf16)
+        sum_ref[:, pl.ds(start, QUARTER)] = near[:, i * QUARTER : (i + 1) * QUARTER] if i < 3 else far
+    hidden = (res_ref[...].astype(f32) + sum_ref[...].astype(bf16).astype(f32)).astype(bf16)
     hidden_ref[...] = hidden
     hidden = hidden.astype(f32)
     inverse = lax.rsqrt(jnp.mean(hidden * hidden, axis=1, keepdims=True) + 1e-6)
@@ -208,37 +285,37 @@
         out_ref[rows, :] = mm(place_ref[rows, :], norm_ref[...]).astype(bf16)
 
 
-def dispatch(parts, residual, gain, place):
+def dispatch(at, parts, residual, gain, place):
     return pl.pallas_call(
         dispatch_kernel,
+        in_specs=[pl.BlockSpec(memory_space=pltpu.SMEM)] + [pl.BlockSpec(memory_space=pltpu.VMEM)] * 8,
         out_shape=(
             jax.ShapeDtypeStruct((ROWS, D), bf16),
             jax.ShapeDtypeStruct((PIECES, QUARTER), bf16),
         ),
-        scratch_shapes=[pltpu.VMEM((4 * ROWS, QUARTER), bf16)],
+        scratch_shapes=[pltpu.VMEM((4 * ROWS, QUARTER), bf16), pltpu.VMEM((ROWS, D), f32)],
         compiler_params=pltpu.CompilerParams(vmem_limit_bytes=VMEM_BYTES),
         cost_estimate=pl.CostEstimate(flops=120_000_000, bytes_accessed=4_000_000, transcendentals=16),
         name="dispatch",
-    )(parts, residual, gain, place)
-
-
-def expert_kernel(x_ref, wi_ref, wo_ref, out_ref, rows_ref, act_ref, back_ref, wi_buf, wo_buf, sems):
-    half = FF // 4
-
-    def copy_in(i):
-        return pltpu.make_async_copy(
-            wi_ref.at[:, pl.ds((i % 2) * FF + (i // 2) * half, half)], wi_buf.at[i], sems.at[i]
-        )
-
-    def copy_out(i):
-        return pltpu.make_async_copy(
-            wo_ref.at[:, pl.ds(i * QUARTER, QUARTER)], wo_buf.at[i], sems.at[8 + i]
-        )
-
-    for i in range(8):
-        copy_in(i).start()
+    )(at, *parts, residual, gain, place)
+
+
+def expert_kernel(x_ref, wi_ref, wo_ref, out_ref, rows_ref, both_ref, act_ref, back_ref, wi_buf, wo_buf, sems):
+    copies = []
+    for i in range(STEPS):
+        source = wi_ref.at[pl.ds(i * DEPTH, DEPTH), :]
+        copies.append(pltpu.make_async_copy(source, wi_buf.at[i], sems.at[i]))
     for i in range(4):
-        copy_out(i).start()
+        source = wo_ref.at[:, pl.ds(i * QUARTER, QUARTER)]
+        copies.append(pltpu.make_async_copy(source, wo_buf.at[i], sems.at[STEPS + i]))
+    ahead = 6
+    for i in range(ahead):
+        copies[i].start()
+
+    def arrive(i):
+        copies[i].wait()
+        if i + ahead < len(copies):
+            copies[i + ahead].start()
 
     def matches(to, frm):
         same_quarter = to // 64 == frm % 8 // 2
@@ -253,15 +330,23 @@
                 quarter * 64 : (quarter + 1) * 64
             ]
 
-    for i in range(4):
-        copy_in(2 * i).wait()
-        copy_in(2 * i + 1).wait()
-        gate = mm(rows_ref[...], wi_buf[2 * i])
-        up = mm(rows_ref[...], wi_buf[2 * i + 1])
-        act_ref[:, i * half : (i + 1) * half] = (jax.nn.silu(gate) * up).astype(bf16)
+    for i in range(STEPS):
+        arrive(i)
+        part = rows_ref[:, i * DEPTH : (i + 1) * DEPTH]
+        for column in range(0, 2 * FF, 512):
+            columns = slice(column, column + 512)
+            more = mm(part, wi_buf[i, :, columns])
+            if i < STEPS - 1:
+                both_ref[:, columns] = more if i == 0 else both_ref[:, columns] + more
+            elif column < FF:
+                both_ref[:, columns] += more
+            else:
+                up = both_ref[:, columns] + more
+                gates = slice(column - FF, column - FF + 512)
+                act_ref[:, gates] = (jax.nn.silu(both_ref[:, gates]) * up).astype(bf16)
 
     for quarter in range(4):
-        copy_out(quarter).wait()
+        arrive(STEPS + quarter)
         result = mm(act_ref[...], wo_buf[quarter]).astype(bf16)
         for b in range(4):
             back_ref[b, quarter * 64 : (quarter + 1) * 64, :] = result[b * 64 : (b + 1) * 64]
@@ -275,20 +360,21 @@
         expert_kernel,
         in_specs=[
             pl.BlockSpec(memory_space=pltpu.VMEM),
-            pl.BlockSpec(memory_space=pl.ANY),
-            pl.BlockSpec(memory_space=pl.ANY),
+            pl.BlockSpec(memory_space=pltpu.HBM),
+            pl.BlockSpec(memory_space=pltpu.HBM),
         ],
         out_specs=pl.BlockSpec(memory_space=pltpu.VMEM),
         out_shape=jax.ShapeDtypeStruct((PIECES, QUARTER), bf16),
         scratch_shapes=[
             pltpu.VMEM((rows, D), bf16),
+            pltpu.VMEM((rows, 2 * FF), f32),
             pltpu.VMEM((rows, FF), bf16),
             pltpu.VMEM((4, 256, QUARTER), bf16),
-            pltpu.VMEM((8, D, FF // 4), bf16),
+            pltpu.VMEM((STEPS, DEPTH, 2 * FF), bf16),
             pltpu.VMEM((4, FF, QUARTER), bf16),
-            pltpu.SemaphoreType.DMA((12,)),
+            pltpu.SemaphoreType.DMA((STEPS + 4,)),
         ],
-        compiler_params=pltpu.CompilerParams(vmem_limit_bytes=VMEM_BYTES),
+        compiler_params=pltpu.CompilerParams(vmem_limit_bytes=48 * 1024 * 1024),
         cost_estimate=pl.CostEstimate(
             flops=2 * rows * 3 * D * FF, bytes_accessed=26_000_000, transcendentals=rows * FF
         ),
@@ -328,27 +414,31 @@
     w_gate_up,
     w_down,
 ):
+    def along_z(block, step):
+        return lax.ppermute(block, "z", [(i, (i - step) % 4) for i in range(4)])
+
+    def other_core(block):
+        return lax.ppermute(block, "core", [(0, 1), (1, 0)])
+
     own = out_proj.T
-    blocks = [own] + [
-        lax.ppermute(own, "z", [(i, (i - step) % 4) for i in range(4)]) for step in (1, 2, 3)
-    ]
-    pairs = []
-    for block in blocks:
-        pairs += [block, lax.ppermute(block, "core", [(0, 1), (1, 0)])]
-    chip = jnp.stack([lax.axis_index("z"), lax.axis_index("core")]).astype(jnp.int32)
-
+    at = jnp.stack([lax.axis_index(name) for name in ("z", "y", "x", "core")]).astype(jnp.int32)
+    next_block, last_block = along_z(own, 1), along_z(own, 3)
     head_out = attention(
         queries.transpose(1, 2, 0),
         cached_latent_rows.transpose(1, 2, 0),
         lengths.reshape(1, REQUESTS),
         value_up_weight,
     )
+    far_head = along_z(head_out, 2)
+    next_block, last_block = hold(next_block, last_block, head_out)
     place, weight = plan(routes, route_scores)
-    shares = project(chip, head_out, pairs)
-    parts = lax.all_to_all(
-        shares.reshape(16, ROWS, D), ("y", "x"), split_axis=0, concat_axis=0, tiled=True
-    )
-    hidden, outgoing = dispatch(parts, residual_in, norm_gain.reshape(1, D), place)
+    own_pair = [own, other_core(own)]
+    near_pairs = own_pair + [next_block, other_core(next_block), last_block, other_core(last_block)]
+    near = exchange("x", project("x", at, head_out, near_pairs))
+    far = exchange("y", project("y", at, far_head, own_pair))
+    far = along_z(total(exchange("x", reduce("x", at, far))), 2)
+    parts = exchange("y", reduce("y", at, near)) + [far]
+    hidden, outgoing = dispatch(at, parts, residual_in, norm_gain.reshape(1, D), place)
     everyone = ("z", "core", "y", "x")
     arrived = lax.all_to_all(
         outgoing.reshape(EXPERTS, 8, QUARTER), everyone, split_axis=0, concat_axis=0, tiled=True

time: 167 us -> 140 us (0.84)
  waiting for transfers between devices: 44 us -> 13.6 us
  starting transfers between devices: 16.3 us -> 27.8 us
  Pallas kernels: 35 us -> 23.6 us
  blocking collectives: 65.4 us -> 69.3 us
    all_to_all x1 -> x0, waiting for transfers between devices: 24.6 us -> none  [local(): lax.all_to_all(shares.reshape(16, ROWS, D), ('y', 'x'), split_axis=0, con...]
    ppermute x7 -> x19, starting transfers between devices: 9.41 us -> 27.8 us  [the longest x12 19.8 us: exchange(): lax.ppermute(parts[step], axis, [(i, (i + step) % 4) for i in range(4)])]
    all_to_all x1 -> x0, starting transfers between devices: 6.9 us -> none  [local(): lax.all_to_all(shares.reshape(16, ROWS, D), ('y', 'x'), split_axis=0, con...]
    ppermute x7 -> x19, waiting for transfers between devices: 19.4 us -> 13.6 us  [the longest x12 6.29 us: exchange(): lax.ppermute(parts[step], axis, [(i, (i + step) % 4) for i in range(4)])]
    all_to_all x1, blocking collectives: 32.7 us -> 37.8 us  [local(): lax.all_to_all(outgoing.reshape(EXPERTS, 8, QUARTER), everyone, split_axi...]
    pallas_call x2 -> x7, Pallas kernels: 9.71 us -> 5.9 us  [the longest x2 2.7 us: project(): pl.pallas_call(functools.partial(project_kernel, first, chips), in_specs=...]
    pallas_call x1, Pallas kernels: 12.9 us -> 10.3 us  [expert(): pl.pallas_call(expert_kernel, in_specs=[pl.BlockSpec(memory_space=pltpu.V...]
    pallas_call x1, Pallas kernels: 7.48 us -> 5.45 us  [attention(): pl.pallas_call(attention_kernel, grid=(REQUESTS // 128,), in_specs=[pl.Bl...]
  transfers between devices with their start and end apart: 8 -> 19, of which waited for: 3 -> 12; matrix products, arithmetic and copies ran while one was open for 2% -> 0% of each run, Pallas kernels for 6% -> 7%
where the time goes in v2:
time: 140 us; the launch traced here: 139 us
  blocking collectives  69.3 us (50%)
  starting transfers between devices  27.8 us (20%)
  Pallas kernels  23.6 us (17%)
  waiting for transfers between devices  13.6 us (10%)
  local copies, waits for them, and re-layouts  4.84 us (3%)
    all_to_all x1, blocking collectives, local(): lax.all_to_all(outgoing.reshape(EXPERTS, 8, QUARTER), everyone, split_axi...  37.8 us
    all_to_all x1, blocking collectives, local(): lax.all_to_all(produced.reshape(EXPERTS, 8, QUARTER), everyone, split_axi...  31.5 us
    ppermute x12, starting transfers between devices, exchange(): lax.ppermute(parts[step], axis, [(i, (i + step) % 4) for i in range(4)])  19.8 us
    pallas_call x1, Pallas kernels, expert(): pl.pallas_call(expert_kernel, in_specs=[pl.BlockSpec(memory_space=pltpu.V...  10.3 us
    ppermute x12, waiting for transfers between devices, exchange(): lax.ppermute(parts[step], axis, [(i, (i + step) % 4) for i in range(4)])  6.29 us
    pallas_call x1, Pallas kernels, attention(): pl.pallas_call(attention_kernel, grid=(REQUESTS // 128,), in_specs=[pl.Bl...  5.45 us
    ppermute x4, waiting for transfers between devices, along_z(): return lax.ppermute(block, 'z', [(i, (i - step) % 4) for i in range(4)])  5.38 us
    ppermute x4, starting transfers between devices, along_z(): return lax.ppermute(block, 'z', [(i, (i - step) % 4) for i in range(4)])  5.29 us
  transfers between devices with their start and end apart: 19, of which 12 were waited for; matrix products, arithmetic and copies ran while one was open for 0% of the time, Pallas kernels for 7%

profile of v2, /device:TPU:1, one launch (start us, length us, event | category | flops | bytes accessed | tf_op | source)
XLA Modules:
  0.0 139.3 jit_solution(2347435742177768310)
XLA Ops:
  0.0 1.4 %collective-permute-start = (bf16[448,512]{1,0:T(8,128)(2,1)}, bf16[448,512]{1,0:T(8,128)(2,1)S(1)}, u32[]{:S(2)}, u32[]{:S(2)}) collective-permute-start(bf16[448,512]{1,0:T(8,128)(2,1)} %bitcast.19), channel_id=1, source_target_pairs={{0,16},{16,0},{1,17},{17,1},{2,18},{18,2},{3,19},{19,3},{4,20},{20... | collective-permute-start | bytes 1376264 | tf_op jit(solution)/shard_map/ppermute | solution.py:421
  1.4 3.8 %collective-permute-start.1 = (bf16[448,512]{1,0:T(8,128)(2,1)}, bf16[448,512]{1,0:T(8,128)(2,1)S(1)}, u32[]{:S(2)}, u32[]{:S(2)}) collective-permute-start(bf16[448,512]{1,0:T(8,128)(2,1)} %bitcast.20), channel_id=1, source_target_pairs={{0,96},{32,0},{64,32},{96,64},{1,97},{33,1},{65,33},{97,65},{2,98}... | collective-permute-start | bytes 1376264 | tf_op jit(solution)/shard_map/ppermute | solution.py:418
  5.3 1.7 %copy-done.3 = bf16[256,8,576]{0,2,1:T(8,128)(2,1)S(1)} copy-done((bf16[256,8,576]{0,2,1:T(8,128)(2,1)S(1)}, bf16[256,8,576]{0,2,1:T(8,128)(2,1)}, u32[]{:S(2)}) %copy-start.3) | copy-done | bytes 2359320
  9.9 5.4 %attention.1.after_ref.head_ref = bf16[256,512]{1,0:T(8,128)(2,1)S(1)} custom-call(bf16[4,576,256]{2,1,0:T(8,128)(2,1)S(1)} %bitcast.26, bf16[8,576,256]{2,1,0:T(8,128)(2,1)S(1)} %bitcast.25, s32[1,256]{1,0:T(1,128)S(1)} %bitcast.27, bf16[4,512,128]{2,1,0:T(8,128)(2,1)S(1)} %copy-done.5), custom_call_target="tpu_custom_call" | custom-call | flops 8999999488 | bytes 4200000 | tf_op jit(solution)/shard_map/attention/pallas_call | solution.py:82
  15.5 3.0 %collective-permute-done.2.last_ref = bf16[448,512]{1,0:T(8,128)(2,1)S(1)} collective-permute-done((bf16[448,512]{1,0:T(8,128)(2,1)}, bf16[448,512]{1,0:T(8,128)(2,1)S(1)}, u32[]{:S(2)}, u32[]{:S(2)}) %collective-permute-start.2) | collective-permute-done | bytes 458784 | tf_op jit(solution)/shard_map/ppermute | solution.py:418
  21.9 1.6 %project_x.1 = (bf16[64,2688]{1,0:T(8,128)(2,1)S(1)}, bf16[64,2688]{1,0:T(8,128)(2,1)S(1)}, bf16[64,2688]{1,0:T(8,128)(2,1)S(1)}, bf16[64,2688]{1,0:T(8,128)(2,1)S(1)}) custom-call(s32[4]{0:T(128)S(1)} %pad_add_fusion.at_ref.place_ref, bf16[256,512]{1,0:T(8,128)(2,1)S(1)} %attention.1.after_ref.head_ref, bf16[448,512]{1,0:T(8,128)(2,1)S(1)} %bitcast.22, ...), custom_call_target="tpu_custom_call" | custom-call | flops 704643072 | bytes 4500000 | tf_op jit(solution)/shard_map/project_x/pallas_call | solution.py:202
  23.6 1.3 collective-permute-start.5
  24.8 2.5 %collective-permute-start.6 = (bf16[64,2688]{1,0:T(8,128)(2,1)S(1)}, bf16[64,2688]{1,0:T(8,128)(2,1)S(1)}, u32[]{:S(2)}, u32[]{:S(2)}) collective-permute-start(bf16[64,2688]{1,0:T(8,128)(2,1)S(1)} %get-tuple-element.31), channel_id=1, source_target_pairs={{0,2},{1,3},{2,0},{3,1},{4,6},{5,7},{6,4},{7,5},{8,10},{9,11},{10,... | collective-permute-start | bytes 1032200 | tf_op jit(solution)/shard_map/ppermute | solution.py:260
  29.9 1.4 collective-permute-start.12
  31.3 2.6 %collective-permute-start.13 = (bf16[64,896]{1,0:T(8,128)(2,1)S(1)}, bf16[64,896]{1,0:T(8,128)(2,1)S(1)}, u32[]{:S(2)}, u32[]{:S(2)}) collective-permute-start(bf16[64,896]{1,0:T(8,128)(2,1)S(1)} %get-tuple-element.39), channel_id=1, source_target_pairs={{0,8},{4,12},{8,0},{12,4},{1,9},{5,13},{9,1},{13,5},{2,10},{6,14},... | collective-permute-start | bytes 344072 | tf_op jit(solution)/shard_map/ppermute | solution.py:260
  34.9 1.7 %collective-permute-start.14 = (bf16[64,896]{1,0:T(8,128)(2,1)S(1)}, bf16[64,896]{1,0:T(8,128)(2,1)S(1)}, u32[]{:S(2)}, u32[]{:S(2)}) collective-permute-start(bf16[64,896]{1,0:T(8,128)(2,1)S(1)} %get-tuple-element.40), channel_id=1, source_target_pairs={{0,12},{4,0},{8,4},{12,8},{1,13},{5,1},{9,5},{13,9},{2,14},{6,2},{... | collective-permute-start | bytes 344072 | tf_op jit(solution)/shard_map/ppermute | solution.py:260
  36.7 1.6 %collective-permute-done.13.refs_2_ = bf16[64,896]{1,0:T(8,128)(2,1)S(1)} collective-permute-done((bf16[64,896]{1,0:T(8,128)(2,1)S(1)}, bf16[64,896]{1,0:T(8,128)(2,1)S(1)}, u32[]{:S(2)}, u32[]{:S(2)}) %collective-permute-start.13) | collective-permute-done | bytes 114720 | tf_op jit(solution)/shard_map/ppermute | solution.py:260
  39.5 1.3 collective-permute-start.15
  40.9 1.6 %collective-permute-done.6.refs_2_ = bf16[64,2688]{1,0:T(8,128)(2,1)S(1)} collective-permute-done((bf16[64,2688]{1,0:T(8,128)(2,1)S(1)}, bf16[64,2688]{1,0:T(8,128)(2,1)S(1)}, u32[]{:S(2)}, u32[]{:S(2)}) %collective-permute-start.6) | collective-permute-done | bytes 344096 | tf_op jit(solution)/shard_map/ppermute | solution.py:260
  43.2 2.8 %collective-permute-start.10 = (bf16[16,2688]{1,0:T(8,128)(2,1)S(1)}, bf16[16,2688]{1,0:T(8,128)(2,1)S(1)}, u32[]{:S(2)}, u32[]{:S(2)}) collective-permute-start(bf16[16,2688]{1,0:T(8,128)(2,1)S(1)} %get-tuple-element.36), channel_id=1, source_target_pairs={{0,12},{4,0},{8,4},{12,8},{1,13},{5,1},{9,5},{13,9},{2,14},{6,2},{... | collective-permute-start | bytes 258056 | tf_op jit(solution)/shard_map/ppermute | solution.py:260
  46.0 1.6 %collective-permute-start.9 = (bf16[16,2688]{1,0:T(8,128)(2,1)S(1)}, bf16[16,2688]{1,0:T(8,128)(2,1)S(1)}, u32[]{:S(2)}, u32[]{:S(2)}) collective-permute-start(bf16[16,2688]{1,0:T(8,128)(2,1)S(1)} %get-tuple-element.35), channel_id=1, source_target_pairs={{0,8},{4,12},{8,0},{12,4},{1,9},{5,13},{9,1},{13,5},{2,10},{6,14},... | collective-permute-start | bytes 258056 | tf_op jit(solution)/shard_map/ppermute | solution.py:260
  47.6 2.1 %collective-permute-start.16 = (bf16[16,896]{1,0:T(8,128)(2,1)S(1)}, bf16[16,896]{1,0:T(8,128)(2,1)S(1)}, u32[]{:S(2)}, u32[]{:S(2)}) collective-permute-start(bf16[16,896]{1,0:T(8,128)(2,1)S(1)} %get-tuple-element.43), channel_id=1, source_target_pairs={{0,2},{1,3},{2,0},{3,1},{4,6},{5,7},{6,4},{7,5},{8,10},{9,11},{10,... | collective-permute-start | bytes 86024 | tf_op jit(solution)/shard_map/ppermute | solution.py:260
  49.7 1.3 collective-permute-start.17
  52.5 1.4 %collective-permute-start.18 = (bf16[16,896]{1,0:T(8,128)(2,1)S(1)}, bf16[16,896]{1,0:T(8,128)(2,1)S(1)}, u32[]{:S(2)}, u32[]{:S(2)}) collective-permute-start(bf16[16,896]{1,0:T(8,128)(2,1)S(1)} %total.1), channel_id=1, source_target_pairs={{0,64},{32,96},{64,0},{96,32},{1,65},{33,97},{65,1},{97,33},{2,66}... | collective-permute-start | bytes 86024 | tf_op jit(solution)/shard_map/ppermute | solution.py:418
  55.0 1.9 %collective-permute-done.18.refs_4_ = bf16[16,896]{1,0:T(8,128)(2,1)S(1)} collective-permute-done((bf16[16,896]{1,0:T(8,128)(2,1)S(1)}, bf16[16,896]{1,0:T(8,128)(2,1)S(1)}, u32[]{:S(2)}, u32[]{:S(2)}) %collective-permute-start.18) | collective-permute-done | bytes 28704 | tf_op jit(solution)/shard_map/ppermute | solution.py:418
  56.8 1.8 %dispatch.1 = (bf16[16,3584]{1,0:T(8,128)(2,1)S(1)}, bf16[1024,896]{1,0:T(8,128)(2,1)S(1)}) custom-call(s32[4]{0:T(128)S(1)} %pad_add_fusion.at_ref.place_ref, bf16[16,2688]{1,0:T(8,128)(2,1)S(1)} %get-tuple-element.33.refs_0_, bf16[16,2688]{1,0:T(8,128)(2,1)S(1)} %collective-permute-done.8.refs_1_, bf16[16,2688]{1,0:T(8,128)(2,1)S(1)} %collective-permute-done.9.refs_2_, ...), custom_call_target="tpu_custom_call" | custom-call | flops 120000000 | bytes 4000000 | tf_op jit(solution)/shard_map/dispatch/pallas_call | solution.py:289
  58.6 37.8 %all_to_all.10 = bf16[128,8,896]{2,1,0:T(8,128)(2,1)S(1)} all-to-all(bf16[128,8,896]{2,1,0:T(8,128)(2,1)S(1)} %bitcast.18), channel_id=1, replica_groups=mesh['z'=4,'core'=2,'y'=4,'x'=4] {'z','core','y','x'}, dimensions={0} | all-to-all | bytes 3670016 | tf_op jit(solution)/shard_map/all_to_all | solution.py:443
  96.5 10.3 %expert.1 = bf16[1024,896]{1,0:T(8,128)(2,1)S(1)} custom-call(bf16[1024,896]{1,0:T(8,128)(2,1)S(1)} %bitcast.15, bf16[3584,2048]{1,0:T(8,128)(2,1)} %bitcast.28, bf16[1024,3584]{1,0:T(8,128)(2,1)} %bitcast.29), custom_call_target="tpu_custom_call" | custom-call | flops 5637144576 | bytes 26000000 | tf_op jit(solution)/shard_map/expert/pallas_call | solution.py:359
  106.8 31.5 %all_to_all.11 = bf16[128,8,896]{2,1,0:T(8,128)(2,1)S(1)} all-to-all(bf16[128,8,896]{2,1,0:T(8,128)(2,1)S(1)} %bitcast.16), channel_id=1, replica_groups=mesh['z'=4,'core'=2,'y'=4,'x'=4] {'z','core','y','x'}, dimensions={0} | all-to-all | bytes 3670016 | tf_op jit(solution)/shard_map/all_to_all | solution.py:447
  (49 shorter events, 15.6 us)
Async XLA Ops:
  0.0 19.9 %collective-permute-start = (bf16[448,512]{1,0:T(8,128)(2,1)}, bf16[448,512]{1,0:T(8,128)(2,1)S(1)}, u32[]{:S(2)}, u32[]{:S(2)}) collective-permute-start(bf16[448,512]{1,0:T(8,128)(2,1)} %bitcast.19), channel_id=1, source_target_pairs={{0,16},{16,0},{1,17},{17,1},{2,18},{18,2},{3,19},{19,3},{4,20},{20... | collective-permute-start | bytes 1376264 | tf_op jit(solution)/shard_map/ppermute | solution.py:421
  1.4 14.1 %collective-permute-start.1 = (bf16[448,512]{1,0:T(8,128)(2,1)}, bf16[448,512]{1,0:T(8,128)(2,1)S(1)}, u32[]{:S(2)}, u32[]{:S(2)}) collective-permute-start(bf16[448,512]{1,0:T(8,128)(2,1)} %bitcast.20), channel_id=1, source_target_pairs={{0,96},{32,0},{64,32},{96,64},{1,97},{33,1},{65,33},{97,65},{2,98}... | collective-permute-start | bytes 1376264 | tf_op jit(solution)/shard_map/ppermute | solution.py:418
  5.3 13.3 %collective-permute-start.2 = (bf16[448,512]{1,0:T(8,128)(2,1)}, bf16[448,512]{1,0:T(8,128)(2,1)S(1)}, u32[]{:S(2)}, u32[]{:S(2)}) collective-permute-start(bf16[448,512]{1,0:T(8,128)(2,1)} %bitcast.21), channel_id=1, source_target_pairs={{0,32},{32,64},{64,96},{96,0},{1,33},{33,65},{65,97},{97,1},{2,34}... | collective-permute-start | bytes 1376264 | tf_op jit(solution)/shard_map/ppermute | solution.py:418
  9.9 11.9 %copy-start = (bf16[512,448]{0,1:T(8,128)(2,1)S(1)}, bf16[512,448]{0,1:T(8,128)(2,1)}, u32[]{:S(2)}) copy-start(bf16[512,448]{0,1:T(8,128)(2,1)} %param.15) | copy-start | bytes 1376260
  18.6 2.6 %collective-permute-start.3 = (bf16[448,512]{1,0:T(8,128)(2,1)S(1)}, bf16[448,512]{1,0:T(8,128)(2,1)S(1)}, u32[]{:S(2)}, u32[]{:S(2)}) collective-permute-start(bf16[448,512]{1,0:T(8,128)(2,1)S(1)} %get-tuple-element.27.refs_2_), channel_id=1, source_target_pairs={{0,16},{16,0},{1,17},{17,1},{2,18},{18,2},{3,19},{19,3},{4,20},{20... | collective-permute-start | bytes 1376264 | tf_op jit(solution)/shard_map/ppermute | solution.py:421
  19.8 2.1 %collective-permute-start.4 = (bf16[448,512]{1,0:T(8,128)(2,1)S(1)}, bf16[448,512]{1,0:T(8,128)(2,1)S(1)}, u32[]{:S(2)}, u32[]{:S(2)}) collective-permute-start(bf16[448,512]{1,0:T(8,128)(2,1)S(1)} %get-tuple-element.28.refs_4_), channel_id=1, source_target_pairs={{0,16},{16,0},{1,17},{17,1},{2,18},{18,2},{3,19},{19,3},{4,20},{20... | collective-permute-start | bytes 1376264 | tf_op jit(solution)/shard_map/ppermute | solution.py:421
  19.9 9.0 %collective-permute-start.11 = (bf16[256,512]{1,0:T(8,128)(2,1)S(1)}, bf16[256,512]{1,0:T(8,128)(2,1)S(1)}, u32[]{:S(2)}, u32[]{:S(2)}) collective-permute-start(bf16[256,512]{1,0:T(8,128)(2,1)S(1)} %attention.1.after_ref.head_ref), channel_id=1, source_target_pairs={{0,64},{32,96},{64,0},{96,32},{1,65},{33,97},{65,1},{97,33},{2,66}... | collective-permute-start | bytes 786440 | tf_op jit(solution)/shard_map/ppermute | solution.py:418
  23.5 30.4 %copy-start.2 = (s32[16,8]{0,1:T(8,128)S(1)}, s32[16,8]{0,1:T(8,128)}, u32[]{:S(2)}) copy-start(s32[16,8]{0,1:T(8,128)} %param.18) | copy-start | bytes 1540
  23.5 30.5 %copy-start.8 = (f32[16,8]{0,1:T(8,128)S(1)}, f32[16,8]{0,1:T(8,128)}, u32[]{:S(2)}) copy-start(f32[16,8]{0,1:T(8,128)} %param.19) | copy-start | bytes 1540
  23.5 30.6 %copy-start.7 = (f32[3584]{0:T(1024)S(1)}, f32[3584]{0:T(1024)}, u32[]{:S(2)}) copy-start(f32[3584]{0:T(1024)} %param.17) | copy-start | bytes 43012
  23.5 33.3 %copy-start.1 = (bf16[16,3584]{1,0:T(8,128)(2,1)S(1)}, bf16[16,3584]{1,0:T(8,128)(2,1)}, u32[]{:S(2)}) copy-start(bf16[16,3584]{1,0:T(8,128)(2,1)} %refs_5_.1) | copy-start | bytes 344068
  23.6 17.3 %collective-permute-start.5 = (bf16[64,2688]{1,0:T(8,128)(2,1)S(1)}, bf16[64,2688]{1,0:T(8,128)(2,1)S(1)}, u32[]{:S(2)}, u32[]{:S(2)}) collective-permute-start(bf16[64,2688]{1,0:T(8,128)(2,1)S(1)} %get-tuple-element.30), channel_id=1, source_target_pairs={{0,1},{1,2},{2,3},{3,0},{4,5},{5,6},{6,7},{7,4},{8,9},{9,10},{10,1... | collective-permute-start | bytes 1032200 | tf_op jit(solution)/shard_map/ppermute | solution.py:260
  24.8 17.6 %collective-permute-start.6 = (bf16[64,2688]{1,0:T(8,128)(2,1)S(1)}, bf16[64,2688]{1,0:T(8,128)(2,1)S(1)}, u32[]{:S(2)}, u32[]{:S(2)}) collective-permute-start(bf16[64,2688]{1,0:T(8,128)(2,1)S(1)} %get-tuple-element.31), channel_id=1, source_target_pairs={{0,2},{1,3},{2,0},{3,1},{4,6},{5,7},{6,4},{7,5},{8,10},{9,11},{10,... | collective-permute-start | bytes 1032200 | tf_op jit(solution)/shard_map/ppermute | solution.py:260
  27.3 15.2 %collective-permute-start.7 = (bf16[64,2688]{1,0:T(8,128)(2,1)S(1)}, bf16[64,2688]{1,0:T(8,128)(2,1)S(1)}, u32[]{:S(2)}, u32[]{:S(2)}) collective-permute-start(bf16[64,2688]{1,0:T(8,128)(2,1)S(1)} %get-tuple-element.32), channel_id=1, source_target_pairs={{0,3},{1,0},{2,1},{3,2},{4,7},{5,4},{6,5},{7,6},{8,11},{9,8},{10,9... | collective-permute-start | bytes 1032200 | tf_op jit(solution)/shard_map/ppermute | solution.py:260
  29.9 5.0 %collective-permute-start.12 = (bf16[64,896]{1,0:T(8,128)(2,1)S(1)}, bf16[64,896]{1,0:T(8,128)(2,1)S(1)}, u32[]{:S(2)}, u32[]{:S(2)}) collective-permute-start(bf16[64,896]{1,0:T(8,128)(2,1)S(1)} %get-tuple-element.38), channel_id=1, source_target_pairs={{0,4},{4,8},{8,12},{12,0},{1,5},{5,9},{9,13},{13,1},{2,6},{6,10},{... | collective-permute-start | bytes 344072 | tf_op jit(solution)/shard_map/ppermute | solution.py:260
  31.3 7.0 %collective-permute-start.13 = (bf16[64,896]{1,0:T(8,128)(2,1)S(1)}, bf16[64,896]{1,0:T(8,128)(2,1)S(1)}, u32[]{:S(2)}, u32[]{:S(2)}) collective-permute-start(bf16[64,896]{1,0:T(8,128)(2,1)S(1)} %get-tuple-element.39), channel_id=1, source_target_pairs={{0,8},{4,12},{8,0},{12,4},{1,9},{5,13},{9,1},{13,5},{2,10},{6,14},... | collective-permute-start | bytes 344072 | tf_op jit(solution)/shard_map/ppermute | solution.py:260
  34.9 4.0 %collective-permute-start.14 = (bf16[64,896]{1,0:T(8,128)(2,1)S(1)}, bf16[64,896]{1,0:T(8,128)(2,1)S(1)}, u32[]{:S(2)}, u32[]{:S(2)}) collective-permute-start(bf16[64,896]{1,0:T(8,128)(2,1)S(1)} %get-tuple-element.40), channel_id=1, source_target_pairs={{0,12},{4,0},{8,4},{12,8},{1,13},{5,1},{9,5},{13,9},{2,14},{6,2},{... | collective-permute-start | bytes 344072 | tf_op jit(solution)/shard_map/ppermute | solution.py:260
  39.5 10.2 %collective-permute-start.15 = (bf16[16,896]{1,0:T(8,128)(2,1)S(1)}, bf16[16,896]{1,0:T(8,128)(2,1)S(1)}, u32[]{:S(2)}, u32[]{:S(2)}) collective-permute-start(bf16[16,896]{1,0:T(8,128)(2,1)S(1)} %get-tuple-element.42), channel_id=1, source_target_pairs={{0,1},{1,2},{2,3},{3,0},{4,5},{5,6},{6,7},{7,4},{8,9},{9,10},{10,1... | collective-permute-start | bytes 86024 | tf_op jit(solution)/shard_map/ppermute | solution.py:260
  43.2 13.6 %collective-permute-start.10 = (bf16[16,2688]{1,0:T(8,128)(2,1)S(1)}, bf16[16,2688]{1,0:T(8,128)(2,1)S(1)}, u32[]{:S(2)}, u32[]{:S(2)}) collective-permute-start(bf16[16,2688]{1,0:T(8,128)(2,1)S(1)} %get-tuple-element.36), channel_id=1, source_target_pairs={{0,12},{4,0},{8,4},{12,8},{1,13},{5,1},{9,5},{13,9},{2,14},{6,2},{... | collective-permute-start | bytes 258056 | tf_op jit(solution)/shard_map/ppermute | solution.py:260
  46.0 10.8 %collective-permute-start.8 = (bf16[16,2688]{1,0:T(8,128)(2,1)S(1)}, bf16[16,2688]{1,0:T(8,128)(2,1)S(1)}, u32[]{:S(2)}, u32[]{:S(2)}) collective-permute-start(bf16[16,2688]{1,0:T(8,128)(2,1)S(1)} %get-tuple-element.34), channel_id=1, source_target_pairs={{0,4},{4,8},{8,12},{12,0},{1,5},{5,9},{9,13},{13,1},{2,6},{6,10},{... | collective-permute-start | bytes 258056 | tf_op jit(solution)/shard_map/ppermute | solution.py:260
  46.0 10.8 %collective-permute-start.9 = (bf16[16,2688]{1,0:T(8,128)(2,1)S(1)}, bf16[16,2688]{1,0:T(8,128)(2,1)S(1)}, u32[]{:S(2)}, u32[]{:S(2)}) collective-permute-start(bf16[16,2688]{1,0:T(8,128)(2,1)S(1)} %get-tuple-element.35), channel_id=1, source_target_pairs={{0,8},{4,12},{8,0},{12,4},{1,9},{5,13},{9,1},{13,5},{2,10},{6,14},... | collective-permute-start | bytes 258056 | tf_op jit(solution)/shard_map/ppermute | solution.py:260
  47.6 4.2 %collective-permute-start.16 = (bf16[16,896]{1,0:T(8,128)(2,1)S(1)}, bf16[16,896]{1,0:T(8,128)(2,1)S(1)}, u32[]{:S(2)}, u32[]{:S(2)}) collective-permute-start(bf16[16,896]{1,0:T(8,128)(2,1)S(1)} %get-tuple-element.43), channel_id=1, source_target_pairs={{0,2},{1,3},{2,0},{3,1},{4,6},{5,7},{6,4},{7,5},{8,10},{9,11},{10,... | collective-permute-start | bytes 86024 | tf_op jit(solution)/shard_map/ppermute | solution.py:260
  49.7 2.7 %collective-permute-start.17 = (bf16[16,896]{1,0:T(8,128)(2,1)S(1)}, bf16[16,896]{1,0:T(8,128)(2,1)S(1)}, u32[]{:S(2)}, u32[]{:S(2)}) collective-permute-start(bf16[16,896]{1,0:T(8,128)(2,1)S(1)} %get-tuple-element.44), channel_id=1, source_target_pairs={{0,3},{1,0},{2,1},{3,2},{4,7},{5,4},{6,5},{7,6},{8,11},{9,8},{10,9... | collective-permute-start | bytes 86024 | tf_op jit(solution)/shard_map/ppermute | solution.py:260
  52.5 4.3 %collective-permute-start.18 = (bf16[16,896]{1,0:T(8,128)(2,1)S(1)}, bf16[16,896]{1,0:T(8,128)(2,1)S(1)}, u32[]{:S(2)}, u32[]{:S(2)}) collective-permute-start(bf16[16,896]{1,0:T(8,128)(2,1)S(1)} %total.1), channel_id=1, source_target_pairs={{0,64},{32,96},{64,0},{96,32},{1,65},{33,97},{65,1},{97,33},{2,66}... | collective-permute-start | bytes 86024 | tf_op jit(solution)/shard_map/ppermute | solution.py:418
  (4 other events, 4.7 us)

commit v3 on v1

v3 whole, which is shorter than its diff:
```python
import jax
import jax.numpy as jnp
from jax import lax
from jax.experimental import pallas as pl
from jax.experimental.pallas import tpu as pltpu
from jax.sharding import Mesh, PartitionSpec as P

D = 3584
FF = 1024
HEADS = 4
LATENT = 512
WIDTH = 576
VALUE = 128
SLOTS = 8
TOP = 8
EXPERTS = 128
ROWS = 16
REQUESTS = 256
QUARTER = D // 4
PIECES = EXPERTS * 8
COLUMNS = 448

score_scale = 0.07216878364870323

f32, bf16 = jnp.float32, jnp.bfloat16
VMEM_BYTES = 16 * 1024 * 1024


def iota(shape, dim):
    return lax.broadcasted_iota(jnp.int32, shape, dim)


def mm(a, b):
    return jnp.dot(a, b, preferred_element_type=f32)


def attention_kernel(q_ref, k_ref, len_ref, up_ref, out_ref, lat_ref):
    def score_step(i, sums):
        rows = pl.ds(i * 16, 16)
        q = [q_ref[h, rows, :].astype(f32) for h in range(HEADS)]
        k = [k_ref[s, rows, :].astype(f32) for s in range(SLOTS)]
        new = []
        for h in range(HEADS):
            for s in range(SLOTS):
                prod = q[h] * k[s]
                new.append(sums[h * SLOTS + s] + (prod[:8] + prod[8:]))
        return tuple(new)

    sums = lax.fori_loop(
        0, WIDTH // 16, score_step, tuple(jnp.zeros((8, 128), f32) for _ in range(HEADS * SLOTS))
    )
    live = iota((SLOTS, 128), 0) < len_ref[...]
    probs = []
    for h in range(HEADS):
        scores = jnp.concatenate(
            [jnp.sum(sums[h * SLOTS + s], axis=0, keepdims=True) for s in range(SLOTS)], axis=0
        )
        scores = jnp.where(live, scores * score_scale, -1e30)
        expo = jnp.exp(scores - jnp.max(scores, axis=0, keepdims=True))
        prob = (expo / jnp.sum(expo, axis=0, keepdims=True)).astype(bf16).astype(f32)
        probs.append([jnp.broadcast_to(prob[s : s + 1], (8, 128)) for s in range(SLOTS)])

    @pl.loop(0, LATENT // 16)
    def _(i):
        rows = pl.ds(i * 16, 16)
        k = [k_ref[s, rows, :].astype(f32) for s in range(SLOTS)]
        for h in range(HEADS):
            low = sum(probs[h][s] * k[s][:8] for s in range(SLOTS))
            high = sum(probs[h][s] * k[s][8:] for s in range(SLOTS))
            lat_ref[h, rows, :] = jnp.concatenate([low, high], axis=0).astype(bf16)

    for h in range(HEADS):
        out_ref[:, h * VALUE : (h + 1) * VALUE] = lax.dot_general(
            lat_ref[h], up_ref[h], (((0,), (0,)), ((), ())), preferred_element_type=f32
        ).astype(bf16)


def attention(q, k, lengths, up):
    return pl.pallas_call(
        attention_kernel,
        grid=(REQUESTS // 128,),
        in_specs=[
            pl.BlockSpec((HEADS, WIDTH, 128), lambda j: (0, 0, j)),
            pl.BlockSpec((SLOTS, WIDTH, 128), lambda j: (0, 0, j)),
            pl.BlockSpec((1, 128), lambda j: (0, j)),
            pl.BlockSpec((HEADS, LATENT, VALUE), lambda j: (0, 0, 0)),
        ],
        out_specs=pl.BlockSpec((128, HEADS * VALUE), lambda j: (j, 0)),
        out_shape=jax.ShapeDtypeStruct((REQUESTS, HEADS * VALUE), bf16),
        scratch_shapes=[pltpu.VMEM((HEADS, LATENT, 128), bf16)],
        compiler_params=pltpu.CompilerParams(vmem_limit_bytes=VMEM_BYTES),
        cost_estimate=pl.CostEstimate(flops=9_000_000_000, bytes_accessed=4_200_000, transcendentals=8192),
        name="attention",
    )(
        pltpu.with_memory_space_constraint(q, pltpu.HBM),
        pltpu.with_memory_space_constraint(k, pltpu.HBM),
        lengths,
        up,
    )


def plan_kernel(at_ref, routes_ref, score_ref, gain_ref, place_ref, weight_ref, gain_out, at_out):
    for i in range(4):
        at_out[i] = at_ref[i]
    gain_out[...] = gain_ref[...]
    routes, scores = routes_ref[...], score_ref[...]
    gates = 2.5 * scores / jnp.sum(scores, axis=0, keepdims=True)
    named = jnp.zeros((EXPERTS, ROWS), f32)
    gate = jnp.zeros((EXPERTS, ROWS), f32)
    for k in range(TOP):
        hit = iota((EXPERTS, ROWS), 0) == routes[k : k + 1, :]
        named += hit.astype(f32)
        gate += jnp.where(hit, gates[k : k + 1, :], 0.0)
    before = (iota((ROWS, ROWS), 0) < iota((ROWS, ROWS), 1)).astype(bf16)
    rank = mm(named.astype(bf16), before)

    spread = (iota((ROWS, 4 * ROWS), 1) % ROWS == iota((ROWS, 4 * ROWS), 0)).astype(bf16)
    expand = (iota((PIECES, EXPERTS), 0) // 8 == iota((PIECES, EXPERTS), 1)).astype(bf16)
    both = []
    for slot in range(2):
        here = jnp.where(rank == slot, named, 0.0).astype(bf16)
        both.append(mm(expand, mm(here, spread).astype(bf16)))
    n = iota((PIECES, 4 * ROWS), 0)
    place = jnp.where(n % 2 == 0, both[0], both[1])
    place_ref[...] = jnp.where(n % 8 // 2 == iota((PIECES, 4 * ROWS), 1) // ROWS, place, 0.0).astype(bf16)

    expand = (iota((EXPERTS, PIECES), 1) // 8 == iota((EXPERTS, PIECES), 0)).astype(bf16)
    n = iota((ROWS, PIECES), 1)
    high, low = [], []
    for slot in range(2):
        part = jnp.where(rank == slot, gate, 0.0).T
        top = part.astype(bf16)
        high.append(mm(top, expand))
        low.append(mm((part - top.astype(f32)).astype(bf16), expand))
    for i, parts in enumerate((high, low)):
        row = jnp.where(n % 2 == 0, parts[0], parts[1])
        for quarter in range(4):
            weight_ref[pl.ds((i * 4 + quarter) * ROWS, ROWS), :] = jnp.where(
                n % 8 // 2 == quarter, row, 0.0
            ).astype(bf16)


def plan(at, routes, scores, gain):
    return pl.pallas_call(
        plan_kernel,
        out_shape=(
            jax.ShapeDtypeStruct((PIECES, 4 * ROWS), bf16),
            jax.ShapeDtypeStruct((8 * ROWS, PIECES), bf16),
            jax.ShapeDtypeStruct((1, D), f32),
            jax.ShapeDtypeStruct((4,), jnp.int32),
        ),
        in_specs=[pl.BlockSpec(memory_space=pltpu.SMEM)] + [pl.BlockSpec(memory_space=pltpu.VMEM)] * 3,
        out_specs=[pl.BlockSpec(memory_space=pltpu.VMEM)] * 3 + [pl.BlockSpec(memory_space=pltpu.SMEM)],
        compiler_params=pltpu.CompilerParams(vmem_limit_bytes=VMEM_BYTES),
        cost_estimate=pl.CostEstimate(flops=60_000_000, bytes_accessed=500_000, transcendentals=0),
        name="plan",
    )(at, routes.T, scores.T, gain)


def fetch_kernel(at_ref, wi_ref, wo_ref, wi_out, wo_out, at_out, sems):
    copies = (
        pltpu.make_async_copy(wi_ref, wi_out, sems.at[0]),
        pltpu.make_async_copy(wo_ref, wo_out, sems.at[1]),
    )
    for copy in copies:
        copy.start()
    for i in range(4):
        at_out[i] = at_ref[i]
    for copy in copies:
        copy.wait()


def fetch(at, w_in, w_out):
    return pl.pallas_call(
        fetch_kernel,
        in_specs=[pl.BlockSpec(memory_space=pltpu.SMEM)] + [pl.BlockSpec(memory_space=pltpu.HBM)] * 2,
        out_specs=[pl.BlockSpec(memory_space=pltpu.VMEM)] * 2 + [pl.BlockSpec(memory_space=pltpu.SMEM)],
        out_shape=[
            pltpu.VMEM(w_in.shape, bf16),
            pltpu.VMEM(w_out.shape, bf16),
            jax.ShapeDtypeStruct((4,), jnp.int32),
        ],
        scratch_shapes=[pltpu.SemaphoreType.DMA((2,))],
        compiler_params=pltpu.CompilerParams(vmem_limit_bytes=VMEM_BYTES),
        cost_estimate=pl.CostEstimate(flops=0, bytes_accessed=26_000_000, transcendentals=0),
        name="fetch",
    )(at, pltpu.with_memory_space_constraint(w_in, pltpu.HBM), pltpu.with_memory_space_constraint(w_out, pltpu.HBM))


def project_kernel(at_ref, head_ref, other_ref, *refs):
    blocks, out_ref, (rows_ref, w_ref) = refs[:4], refs[4], refs[5:]
    for i in range(REQUESTS // ROWS):
        rows = slice(i * ROWS, (i + 1) * ROWS)
        rows_ref[2 * i * ROWS : (2 * i + 1) * ROWS, :] = head_ref[rows, :]
        rows_ref[(2 * i + 1) * ROWS : (2 * i + 2) * ROWS, :] = other_ref[rows, :]
    for i in range(4):
        w_ref[i * COLUMNS : (i + 1) * COLUMNS, :] = blocks[i][...]
    for i in range(2):
        columns = slice(i * 2 * COLUMNS, (i + 1) * 2 * COLUMNS)
        out_ref[:, columns] = lax.dot_general(
            rows_ref[...], w_ref[columns, :], (((1,), (1,)), ((), ())), preferred_element_type=f32
        ).astype(bf16)


def project(at, head_out, other_head, blocks):
    return pl.pallas_call(
        project_kernel,
        in_specs=[pl.BlockSpec(memory_space=pltpu.SMEM)] + [pl.BlockSpec(memory_space=pltpu.VMEM)] * 6,
        out_specs=pl.BlockSpec(memory_space=pltpu.VMEM),
        out_shape=jax.ShapeDtypeStruct((2 * REQUESTS, 4 * COLUMNS), bf16),
        scratch_shapes=[
            pltpu.VMEM((2 * REQUESTS, HEADS * VALUE), bf16),
            pltpu.VMEM((4 * COLUMNS, HEADS * VALUE), bf16),
        ],
        compiler_params=pltpu.CompilerParams(vmem_limit_bytes=VMEM_BYTES),
        cost_estimate=pl.CostEstimate(flops=2 * REQUESTS * 512 * D, bytes_accessed=4_500_000, transcendentals=0),
        name="project",
    )(at, head_out, other_head, *blocks)


def total_kernel(parts_ref, own_ref, other_ref):
    for out_ref, start in ((own_ref, 0), (other_ref, ROWS)):
        rows = slice(start, start + ROWS)
        total = parts_ref[0, rows, :].astype(f32)
        for i in range(1, parts_ref.shape[0]):
            total += parts_ref[i, rows, :].astype(f32)
        out_ref[...] = total.astype(bf16)


def total(parts):
    return pl.pallas_call(
        total_kernel,
        out_shape=[jax.ShapeDtypeStruct((ROWS, 4 * COLUMNS), bf16)] * 2,
        compiler_params=pltpu.CompilerParams(vmem_limit_bytes=VMEM_BYTES),
        cost_estimate=pl.CostEstimate(flops=1_000_000, bytes_accessed=2_000_000, transcendentals=0),
        name="total",
    )(parts)


def dispatch_kernel(
    at_ref, own_ref, other_ref, res_ref, gain_ref, place_ref, hidden_ref, out_ref, norm_ref, sum_ref
):
    z, core = at_ref[0], at_ref[3]
    own, other = own_ref[...].astype(f32), other_ref[...].astype(f32)
    even = jnp.where(core == 0, own, other)
    odd = jnp.where(core == 0, other, own)
    for step in range(4):
        columns = slice(step * COLUMNS, (step + 1) * COLUMNS)
        start = pl.multiple_of(lax.rem(z + step, 4) * QUARTER, 128)
        sum_ref[:, pl.ds(start, QUARTER)] = jnp.concatenate([even[:, columns], odd[:, columns]], axis=1)
    hidden = (res_ref[...].astype(f32) + sum_ref[...]).astype(bf16)
    hidden_ref[...] = hidden
    hidden = hidden.astype(f32)
    inverse = lax.rsqrt(jnp.mean(hidden * hidden, axis=1, keepdims=True) + 1e-6)
    normed = (hidden * inverse * gain_ref[...]).astype(bf16)
    for quarter in range(4):
        norm_ref[pl.ds(quarter * ROWS, ROWS), :] = normed[:, quarter * QUARTER : (quarter + 1) * QUARTER]

    @pl.loop(0, 4)
    def _(i):
        rows = pl.ds(i * (PIECES // 4), PIECES // 4)
        out_ref[rows, :] = mm(place_ref[rows, :], norm_ref[...]).astype(bf16)


def dispatch(at, own, other, residual, gain, place):
    return pl.pallas_call(
        dispatch_kernel,
        in_specs=[pl.BlockSpec(memory_space=pltpu.SMEM)] + [pl.BlockSpec(memory_space=pltpu.VMEM)] * 5,
        out_shape=(
            jax.ShapeDtypeStruct((ROWS, D), bf16),
            jax.ShapeDtypeStruct((PIECES, QUARTER), bf16),
        ),
        scratch_shapes=[pltpu.VMEM((4 * ROWS, QUARTER), bf16), pltpu.VMEM((ROWS, D), f32)],
        compiler_params=pltpu.CompilerParams(vmem_limit_bytes=VMEM_BYTES),
        cost_estimate=pl.CostEstimate(flops=120_000_000, bytes_accessed=4_000_000, transcendentals=16),
        name="dispatch",
    )(at, own, other, residual, gain, place)


def expert_kernel(x_ref, wi_ref, wo_ref, out_ref, rows_ref, act_ref, back_ref):
    half = FF // 4

    def matches(to, frm):
        same_quarter = to // 64 == frm % 8 // 2
        return (same_quarter & (to % 64 // 2 == frm // 8) & (to % 2 == frm % 2)).astype(bf16)

    sort = matches(iota((256, 256), 0), iota((256, 256), 1))
    unsort = matches(iota((256, 256), 1), iota((256, 256), 0))
    for b in range(4):
        sorted_rows = mm(sort, x_ref[b * 256 : (b + 1) * 256, :]).astype(bf16)
        for quarter in range(4):
            rows_ref[b * 64 : (b + 1) * 64, quarter * QUARTER : (quarter + 1) * QUARTER] = sorted_rows[
                quarter * 64 : (quarter + 1) * 64
            ]

    for i in range(4):
        gate = mm(rows_ref[...], wi_ref[:, i * half : (i + 1) * half])
        up = mm(rows_ref[...], wi_ref[:, FF + i * half : FF + (i + 1) * half])
        act_ref[:, i * half : (i + 1) * half] = (jax.nn.silu(gate) * up).astype(bf16)

    for quarter in range(4):
        result = mm(act_ref[...], wo_ref[:, quarter * QUARTER : (quarter + 1) * QUARTER]).astype(bf16)
        for b in range(4):
            back_ref[b, quarter * 64 : (quarter + 1) * 64, :] = result[b * 64 : (b + 1) * 64]
    for b in range(4):
        out_ref[b * 256 : (b + 1) * 256, :] = mm(unsort, back_ref[b]).astype(bf16)


def expert(pieces, w_in, w_out):
    rows = 2 * EXPERTS
    return pl.pallas_call(
        expert_kernel,
        in_specs=[pl.BlockSpec(memory_space=pltpu.VMEM)] * 3,
        out_specs=pl.BlockSpec(memory_space=pltpu.VMEM),
        out_shape=jax.ShapeDtypeStruct((PIECES, QUARTER), bf16),
        scratch_shapes=[
            pltpu.VMEM((rows, D), bf16),
            pltpu.VMEM((rows, FF), bf16),
            pltpu.VMEM((4, 256, QUARTER), bf16),
        ],
        compiler_params=pltpu.CompilerParams(vmem_limit_bytes=VMEM_BYTES),
        cost_estimate=pl.CostEstimate(
            flops=2 * rows * 3 * D * FF, bytes_accessed=26_000_000, transcendentals=rows * FF
        ),
        name="expert",
    )(
        pieces,
        w_in,
        w_out,
    )


def combine_kernel(back_ref, weight_ref, hidden_ref, out_ref):
    both = mm(weight_ref[...], back_ref[...])
    for quarter in range(4):
        columns = slice(quarter * QUARTER, (quarter + 1) * QUARTER)
        rows = slice(quarter * ROWS, (quarter + 1) * ROWS)
        low_rows = slice((4 + quarter) * ROWS, (5 + quarter) * ROWS)
        out_ref[:, columns] = (hidden_ref[:, columns].astype(f32) + (both[rows] + both[low_rows])).astype(bf16)


def combine(back, weight, hidden):
    return pl.pallas_call(
        combine_kernel,
        out_shape=jax.ShapeDtypeStruct((ROWS, D), bf16),
        compiler_params=pltpu.CompilerParams(vmem_limit_bytes=VMEM_BYTES),
        cost_estimate=pl.CostEstimate(flops=240_000_000, bytes_accessed=2_400_000, transcendentals=0),
        name="combine",
    )(back, weight, hidden)


def local(
    queries,
    cached_latent_rows,
    lengths,
    value_up_weight,
    out_proj,
    residual_in,
    norm_gain,
    routes,
    route_scores,
    w_gate_up,
    w_down,
):
    own = out_proj.T
    others = [lax.ppermute(own, "z", [(i, (i - step) % 4) for i in range(4)]) for step in (1, 2, 3)]
    at = jnp.stack([lax.axis_index(name) for name in ("z", "y", "x", "core")]).astype(jnp.int32)

    def other_core(block):
        return lax.ppermute(block, "core", [(0, 1), (1, 0)])

    head_out = attention(
        queries.transpose(1, 2, 0),
        cached_latent_rows.transpose(1, 2, 0),
        lengths.reshape(1, REQUESTS),
        value_up_weight,
    )
    place, weight, gain, at = plan(at, routes, route_scores, norm_gain.reshape(1, D))
    w_in, w_out, at = fetch(at, w_gate_up[0], w_down[0])
    shares = project(at, head_out, other_core(head_out), (own, *others))
    parts = lax.all_to_all(
        shares.reshape(16, 2 * ROWS, 4 * COLUMNS), ("y", "x"), split_axis=0, concat_axis=0, tiled=True
    )
    own_total, other_total = total(parts)
    hidden, outgoing = dispatch(at, own_total, other_core(other_total), residual_in, gain, place)
    everyone = ("z", "core", "y", "x")
    arrived = lax.all_to_all(
        outgoing.reshape(EXPERTS, 8, QUARTER), everyone, split_axis=0, concat_axis=0, tiled=True
    )
    produced = expert(arrived.reshape(PIECES, QUARTER), w_in, w_out)
    returned = lax.all_to_all(
        produced.reshape(EXPERTS, 8, QUARTER), everyone, split_axis=0, concat_axis=0, tiled=True
    )
    return combine(returned.reshape(PIECES, QUARTER), weight, hidden)


def solution(mesh):
    fine = Mesh(mesh.devices.reshape(4, 2, 4, 4), ("z", "core", "y", "x"))
    dp, ex, both = ("z", "core"), ("y", "x"), ("z", "core", "y", "x")
    in_specs = (
        P(dp, ex, None),
        P(dp, None, None),
        P(dp),
        P(ex, None, None),
        P(ex, dp),
        P(both, None),
        P(),
        P(both, None),
        P(both, None),
        P(both, None, None),
        P(both, None, None),
    )
    return jax.shard_map(local, mesh=fine, in_specs=in_specs, out_specs=P(both, None), check_vma=False)
```

time: 167 us -> 136 us (0.81)
  waiting for transfers between devices: 44 us -> 0.9 us
  blocking collectives: 65.4 us -> 93.9 us
  Pallas kernels: 35 us -> 28.4 us
  starting transfers between devices: 16.3 us -> 10.7 us
  local copies, waits for them, and re-layouts: 4.98 us -> 1.75 us
    all_to_all x0 -> x1, blocking collectives: none -> 30.6 us  [local(): lax.all_to_all(shares.reshape(16, 2 * ROWS, 4 * COLUMNS), ('y', 'x'), spl...]
    all_to_all x1 -> x0, waiting for transfers between devices: 24.6 us -> none  [local(): lax.all_to_all(shares.reshape(16, ROWS, D), ('y', 'x'), split_axis=0, con...]
    ppermute x3, waiting for transfers between devices: 19.4 us -> 0.01 us  [local(): lax.ppermute(own, 'z', [(i, (i - step) % 4) for i in range(4)])]
    all_to_all x1 -> x0, starting transfers between devices: 6.9 us -> none  [local(): lax.all_to_all(shares.reshape(16, ROWS, D), ('y', 'x'), split_axis=0, con...]
    pallas_call x1 -> x3, Pallas kernels: 4.37 us -> 10.4 us  [the longest x1 8.41 us: fetch(): pl.pallas_call(fetch_kernel, in_specs=[pl.BlockSpec(memory_space=pltpu.SM...]
    pallas_call x1, Pallas kernels: 12.9 us -> 7.35 us  [expert(): pl.pallas_call(expert_kernel, in_specs=[pl.BlockSpec(memory_space=pltpu.V...]
    pallas_call x1, Pallas kernels: 5.35 us -> 1.83 us  [project(): pl.pallas_call(project_kernel, in_specs=[pl.BlockSpec(memory_space=pltpu....]
    unnamed x24 -> x14, local copies, waits for them, and re-layouts: 4.37 us -> 1.74 us
  transfers between devices with their start and end apart: 8 -> 5, of which waited for: 3 -> 1; matrix products, arithmetic and copies ran while one was open for 2% -> 0% of each run, Pallas kernels for 6% -> 12%
where the time goes in v3:
time: 136 us
  blocking collectives  93.9 us (69%)
  Pallas kernels  28.4 us (21%)
  starting transfers between devices  10.7 us (8%)
  local copies, waits for them, and re-layouts  1.75 us (1%)
    all_to_all x1, blocking collectives, local(): lax.all_to_all(outgoing.reshape(EXPERTS, 8, QUARTER), everyone, split_axi...  31.8 us
    all_to_all x1, blocking collectives, local(): lax.all_to_all(produced.reshape(EXPERTS, 8, QUARTER), everyone, split_axi...  31.5 us
    all_to_all x1, blocking collectives, local(): lax.all_to_all(shares.reshape(16, 2 * ROWS, 4 * COLUMNS), ('y', 'x'), spl...  30.6 us
    pallas_call x1, Pallas kernels, fetch(): pl.pallas_call(fetch_kernel, in_specs=[pl.BlockSpec(memory_space=pltpu.SM...  8.41 us
    pallas_call x1, Pallas kernels, expert(): pl.pallas_call(expert_kernel, in_specs=[pl.BlockSpec(memory_space=pltpu.V...  7.35 us
    ppermute x3, starting transfers between devices, local(): lax.ppermute(own, 'z', [(i, (i - step) % 4) for i in range(4)])  6.5 us
    pallas_call x1, Pallas kernels, attention(): pl.pallas_call(attention_kernel, grid=(REQUESTS // 128,), in_specs=[pl.Bl...  6.32 us
    ppermute x2, starting transfers between devices, other_core(): return lax.ppermute(block, 'core', [(0, 1), (1, 0)])  4.22 us
  transfers between devices with their start and end apart: 5, of which 1 were waited for; matrix products, arithmetic and copies ran while one was open for 0% of the time, Pallas kernels for 12%

profile of v3, /device:TPU:1, one launch (start us, length us, event | category | flops | bytes accessed | tf_op | source)
XLA Modules:
  0.0 135.8 jit_solution(9473403639858613935)
XLA Ops:
  0.0 2.5 %collective-permute-start.3 = (bf16[448,512]{1,0:T(8,128)(2,1)}, bf16[448,512]{1,0:T(8,128)(2,1)S(1)}, u32[]{:S(2)}, u32[]{:S(2)}) collective-permute-start(bf16[448,512]{1,0:T(8,128)(2,1)} %bitcast.22), channel_id=1, source_target_pairs={{0,32},{32,64},{64,96},{96,0},{1,33},{33,65},{65,97},{97,1},{2,34}... | collective-permute-start | bytes 1376264 | tf_op jit(solution)/shard_map/ppermute | solution.py:366
  2.5 3.3 %collective-permute-start.2 = (bf16[448,512]{1,0:T(8,128)(2,1)}, bf16[448,512]{1,0:T(8,128)(2,1)S(1)}, u32[]{:S(2)}, u32[]{:S(2)}) collective-permute-start(bf16[448,512]{1,0:T(8,128)(2,1)} %bitcast.23), channel_id=1, source_target_pairs={{0,64},{32,96},{64,0},{96,32},{1,65},{33,97},{65,1},{97,33},{2,66}... | collective-permute-start | bytes 1376264 | tf_op jit(solution)/shard_map/ppermute | solution.py:366
  5.8 0.7 collective-permute-start.1
  6.5 1.0 copy-done.2
  7.5 0.7 copy-done.5
  8.2 6.3 %attention.1.head_ref = bf16[256,512]{1,0:T(8,128)(2,1)S(1)} custom-call(bf16[4,576,256]{2,1,0:T(8,128)(2,1)} %bitcast.32, bf16[8,576,256]{2,1,0:T(8,128)(2,1)} %bitcast.31, s32[1,256]{1,0:T(1,128)S(1)} %bitcast.28, bf16[4,512,128]{2,1,0:T(8,128)(2,1)S(1)} %copy-done.2), custom_call_target="tpu_custom_call" | custom-call | flops 8999999488 | bytes 4200000 | tf_op jit(solution)/shard_map/attention/pallas_call | solution.py:79
  14.6 1.6 %collective-permute-start = (bf16[256,512]{1,0:T(8,128)(2,1)S(1)}, bf16[256,512]{1,0:T(8,128)(2,1)S(1)}, u32[]{:S(2)}, u32[]{:S(2)}) collective-permute-start(bf16[256,512]{1,0:T(8,128)(2,1)S(1)} %attention.1.head_ref), channel_id=1, source_target_pairs={{0,16},{16,0},{1,17},{17,1},{2,18},{18,2},{3,19},{19,3},{4,20},{20... | collective-permute-start | bytes 786440 | tf_op jit(solution)/shard_map/ppermute | solution.py:370
  16.2 0.1 pad_add_fusion.at_ref
  16.3 1.3 plan.1
  17.6 0.0 copy-start
  17.6 8.4 %fetch.1 = (bf16[3584,2048]{1,0:T(8,128)(2,1)S(1)}, bf16[1024,3584]{1,0:T(8,128)(2,1)S(1)}, s32[4]{0:T(128)S(1)}) custom-call(s32[4]{0:T(128)S(1)} %get-tuple-element.16.at_ref, bf16[3584,2048]{1,0:T(8,128)(2,1)} %bitcast.29, bf16[1024,3584]{1,0:T(8,128)(2,1)} %bitcast.30), custom_call_target="tpu_custom_call" | custom-call | bytes 26000000 | tf_op jit(solution)/shard_map/fetch/pallas_call | solution.py:174
  26.0 0.0 collective-permute-done.other_ref
  26.0 0.0 collective-permute-done.2.refs_2_
  26.1 0.0 collective-permute-done.1.refs_1_
  26.1 1.8 %project.1 = bf16[512,1792]{1,0:T(8,128)(2,1)S(1)} custom-call(s32[4]{0:T(128)S(1)} %get-tuple-element.17.at_ref, bf16[256,512]{1,0:T(8,128)(2,1)S(1)} %attention.1.head_ref, bf16[256,512]{1,0:T(8,128)(2,1)S(1)} %collective-permute-done.other_ref, bf16[448,512]{1,0:T(8,128)(2,1)S(1)} %bitcast.25, bf16[448,512]{1,0:T(8,128)(2,1)S(1)} %collective-permute-done.1.refs_1_, ...), custom_call_target="tpu_custom_call" | custom-call | flops 939524096 | bytes 4500000 | tf_op jit(solution)/shard_map/project/pallas_call | solution.py:206
  27.9 30.6 %all_to_all.15.parts_ref = bf16[16,32,1792]{2,1,0:T(8,128)(2,1)S(1)} all-to-all(bf16[16,32,1792]{2,1,0:T(8,128)(2,1)S(1)} %bitcast.20), channel_id=1, replica_groups=mesh['z'=4,'core'=2,'y'=4,'x'=4] {'y','x'}, dimensions={0} | all-to-all | bytes 3670016 | tf_op jit(solution)/shard_map/all_to_all | solution.py:381
  58.5 0.2 total.1
  58.8 2.6 %collective-permute-start.4 = (bf16[16,1792]{1,0:T(8,128)(2,1)S(1)}, bf16[16,1792]{1,0:T(8,128)(2,1)S(1)}, u32[]{:S(2)}, u32[]{:S(2)}) collective-permute-start(bf16[16,1792]{1,0:T(8,128)(2,1)S(1)} %get-tuple-element.19), channel_id=1, source_target_pairs={{0,16},{16,0},{1,17},{17,1},{2,18},{18,2},{3,19},{19,3},{4,20},{20... | collective-permute-start | bytes 172040 | tf_op jit(solution)/shard_map/ppermute | solution.py:370
  61.4 0.9 collective-permute-done.4.other_ref
  62.3 1.8 %dispatch.1 = (bf16[16,3584]{1,0:T(8,128)(2,1)S(1)}, bf16[1024,896]{1,0:T(8,128)(2,1)S(1)}) custom-call(s32[4]{0:T(128)S(1)} %get-tuple-element.17.at_ref, bf16[16,1792]{1,0:T(8,128)(2,1)S(1)} %get-tuple-element.18.own_ref, bf16[16,1792]{1,0:T(8,128)(2,1)S(1)} %collective-permute-done.4.other_ref, bf16[16,3584]{1,0:T(8,128)(2,1)S(1)} %copy-done.1, ...), custom_call_target="tpu_custom_call" | custom-call | flops 120000000 | bytes 4000000 | tf_op jit(solution)/shard_map/dispatch/pallas_call | solution.py:266
  64.1 31.8 %all_to_all.16 = bf16[128,8,896]{2,1,0:T(8,128)(2,1)S(1)} all-to-all(bf16[128,8,896]{2,1,0:T(8,128)(2,1)S(1)} %bitcast.21), channel_id=1, replica_groups=mesh['z'=4,'core'=2,'y'=4,'x'=4] {'z','core','y','x'}, dimensions={0} | all-to-all | bytes 3670016 | tf_op jit(solution)/shard_map/all_to_all | solution.py:387
  95.9 7.3 %expert.1 = bf16[1024,896]{1,0:T(8,128)(2,1)S(1)} custom-call(bf16[1024,896]{1,0:T(8,128)(2,1)S(1)} %bitcast.17, bf16[3584,2048]{1,0:T(8,128)(2,1)S(1)} %get-tuple-element.23.wi_ref, bf16[1024,3584]{1,0:T(8,128)(2,1)S(1)} %get-tuple-element.24.wo_ref), custom_call_target="tpu_custom_call" | custom-call | flops 5637144576 | bytes 26000000 | tf_op jit(solution)/shard_map/expert/pallas_call | solution.py:311
  103.2 31.5 %all_to_all.17 = bf16[128,8,896]{2,1,0:T(8,128)(2,1)S(1)} all-to-all(bf16[128,8,896]{2,1,0:T(8,128)(2,1)S(1)} %bitcast.18), channel_id=1, replica_groups=mesh['z'=4,'core'=2,'y'=4,'x'=4] {'z','core','y','x'}, dimensions={0} | all-to-all | bytes 3670016 | tf_op jit(solution)/shard_map/all_to_all | solution.py:391
  134.7 1.1 combine.1
  (13 shorter events, 0.0 us)
Async XLA Ops:
  0.0 26.0 %collective-permute-start.3 = (bf16[448,512]{1,0:T(8,128)(2,1)}, bf16[448,512]{1,0:T(8,128)(2,1)S(1)}, u32[]{:S(2)}, u32[]{:S(2)}) collective-permute-start(bf16[448,512]{1,0:T(8,128)(2,1)} %bitcast.22), channel_id=1, source_target_pairs={{0,32},{32,64},{64,96},{96,0},{1,33},{33,65},{65,97},{97,1},{2,34}... | collective-permute-start | bytes 1376264 | tf_op jit(solution)/shard_map/ppermute | solution.py:366
  2.5 23.6 %collective-permute-start.2 = (bf16[448,512]{1,0:T(8,128)(2,1)}, bf16[448,512]{1,0:T(8,128)(2,1)S(1)}, u32[]{:S(2)}, u32[]{:S(2)}) collective-permute-start(bf16[448,512]{1,0:T(8,128)(2,1)} %bitcast.23), channel_id=1, source_target_pairs={{0,64},{32,96},{64,0},{96,32},{1,65},{33,97},{65,1},{97,33},{2,66}... | collective-permute-start | bytes 1376264 | tf_op jit(solution)/shard_map/ppermute | solution.py:366
  5.8 20.3 %collective-permute-start.1 = (bf16[448,512]{1,0:T(8,128)(2,1)}, bf16[448,512]{1,0:T(8,128)(2,1)S(1)}, u32[]{:S(2)}, u32[]{:S(2)}) collective-permute-start(bf16[448,512]{1,0:T(8,128)(2,1)} %bitcast.24), channel_id=1, source_target_pairs={{0,96},{32,0},{64,32},{96,64},{1,97},{33,1},{65,33},{97,65},{2,98}... | collective-permute-start | bytes 1376264 | tf_op jit(solution)/shard_map/ppermute | solution.py:366
  6.5 1.0 copy-start.2
  7.5 0.7 copy-start.5
  8.2 7.9 %copy-start.6 = (f32[3584]{0:T(1024)S(1)}, f32[3584]{0:T(1024)}, u32[]{:S(2)}) copy-start(f32[3584]{0:T(1024)} %param.17) | copy-start | bytes 43012
  8.2 8.0 %copy-start.3 = (s32[16,8]{0,1:T(8,128)S(1)}, s32[16,8]{0,1:T(8,128)}, u32[]{:S(2)}) copy-start(s32[16,8]{0,1:T(8,128)} %param.18) | copy-start | bytes 1540
  8.2 8.0 %copy-start.4 = (f32[16,8]{0,1:T(8,128)S(1)}, f32[16,8]{0,1:T(8,128)}, u32[]{:S(2)}) copy-start(f32[16,8]{0,1:T(8,128)} %param.19) | copy-start | bytes 1540
  14.6 11.5 %collective-permute-start = (bf16[256,512]{1,0:T(8,128)(2,1)S(1)}, bf16[256,512]{1,0:T(8,128)(2,1)S(1)}, u32[]{:S(2)}, u32[]{:S(2)}) collective-permute-start(bf16[256,512]{1,0:T(8,128)(2,1)S(1)} %attention.1.head_ref), channel_id=1, source_target_pairs={{0,16},{16,0},{1,17},{17,1},{2,18},{18,2},{3,19},{19,3},{4,20},{20... | collective-permute-start | bytes 786440 | tf_op jit(solution)/shard_map/ppermute | solution.py:370
  17.6 8.5 %copy-start = (bf16[512,448]{0,1:T(8,128)(2,1)S(1)}, bf16[512,448]{0,1:T(8,128)(2,1)}, u32[]{:S(2)}) copy-start(bf16[512,448]{0,1:T(8,128)(2,1)} %param.15) | copy-start | bytes 1376260
  58.5 3.8 %copy-start.1 = (bf16[16,3584]{1,0:T(8,128)(2,1)S(1)}, bf16[16,3584]{1,0:T(8,128)(2,1)}, u32[]{:S(2)}) copy-start(bf16[16,3584]{1,0:T(8,128)(2,1)} %res_ref.1) | copy-start | bytes 344068
  58.8 3.5 %collective-permute-start.4 = (bf16[16,1792]{1,0:T(8,128)(2,1)S(1)}, bf16[16,1792]{1,0:T(8,128)(2,1)S(1)}, u32[]{:S(2)}, u32[]{:S(2)}) collective-permute-start(bf16[16,1792]{1,0:T(8,128)(2,1)S(1)} %get-tuple-element.19), channel_id=1, source_target_pairs={{0,16},{16,0},{1,17},{17,1},{2,18},{18,2},{3,19},{19,3},{4,20},{20... | collective-permute-start | bytes 172040 | tf_op jit(solution)/shard_map/ppermute | solution.py:370

commit v4 on v3

--- a/solution.py
+++ b/solution.py
@@ -19,6 +19,7 @@
 QUARTER = D // 4
 PIECES = EXPERTS * 8
 COLUMNS = 448
+CHIPS = (0, 2, 1, 3)
 
 score_scale = 0.07216878364870323
 
@@ -99,10 +100,7 @@
     )
 
 
-def plan_kernel(at_ref, routes_ref, score_ref, gain_ref, place_ref, weight_ref, gain_out, at_out):
-    for i in range(4):
-        at_out[i] = at_ref[i]
-    gain_out[...] = gain_ref[...]
+def plan_kernel(routes_ref, score_ref, place_ref, weight_ref):
     routes, scores = routes_ref[...], score_ref[...]
     gates = 2.5 * scores / jnp.sum(scores, axis=0, keepdims=True)
     named = jnp.zeros((EXPERTS, ROWS), f32)
@@ -140,55 +138,53 @@
             ).astype(bf16)
 
 
-def plan(at, routes, scores, gain):
+def plan(routes, scores):
     return pl.pallas_call(
         plan_kernel,
         out_shape=(
             jax.ShapeDtypeStruct((PIECES, 4 * ROWS), bf16),
             jax.ShapeDtypeStruct((8 * ROWS, PIECES), bf16),
-            jax.ShapeDtypeStruct((1, D), f32),
-            jax.ShapeDtypeStruct((4,), jnp.int32),
         ),
-        in_specs=[pl.BlockSpec(memory_space=pltpu.SMEM)] + [pl.BlockSpec(memory_space=pltpu.VMEM)] * 3,
-        out_specs=[pl.BlockSpec(memory_space=pltpu.VMEM)] * 3 + [pl.BlockSpec(memory_space=pltpu.SMEM)],
         compiler_params=pltpu.CompilerParams(vmem_limit_bytes=VMEM_BYTES),
         cost_estimate=pl.CostEstimate(flops=60_000_000, bytes_accessed=500_000, transcendentals=0),
         name="plan",
-    )(at, routes.T, scores.T, gain)
-
-
-def fetch_kernel(at_ref, wi_ref, wo_ref, wi_out, wo_out, at_out, sems):
-    copies = (
-        pltpu.make_async_copy(wi_ref, wi_out, sems.at[0]),
-        pltpu.make_async_copy(wo_ref, wo_out, sems.at[1]),
-    )
+    )(routes.T, scores.T)
+
+
+def fetch_kernel(gain_ref, wi_ref, wo_ref, wi_out, wo_out, gain_out, sems):
+    gain_out[...] = gain_ref[...]
+    copies = []
+    for source, target, pieces in ((wi_ref, wi_out, 8), (wo_ref, wo_out, 4)):
+        depth = source.shape[0] // pieces
+        for i in range(pieces):
+            rows = pl.ds(i * depth, depth)
+            copies.append(pltpu.make_async_copy(source.at[rows, :], target.at[rows, :], sems.at[len(copies)]))
     for copy in copies:
         copy.start()
-    for i in range(4):
-        at_out[i] = at_ref[i]
     for copy in copies:
         copy.wait()
 
 
-def fetch(at, w_in, w_out):
+def fetch(gain, w_in, w_out):
+    in_hbm = [pltpu.with_memory_space_constraint(w, pltpu.HBM) for w in (w_in, w_out)]
     return pl.pallas_call(
         fetch_kernel,
-        in_specs=[pl.BlockSpec(memory_space=pltpu.SMEM)] + [pl.BlockSpec(memory_space=pltpu.HBM)] * 2,
-        out_specs=[pl.BlockSpec(memory_space=pltpu.VMEM)] * 2 + [pl.BlockSpec(memory_space=pltpu.SMEM)],
+        in_specs=[pl.BlockSpec(memory_space=space) for space in (pltpu.VMEM, pltpu.HBM, pltpu.HBM)],
+        out_specs=[pl.BlockSpec(memory_space=pltpu.VMEM)] * 3,
         out_shape=[
             pltpu.VMEM(w_in.shape, bf16),
             pltpu.VMEM(w_out.shape, bf16),
-            jax.ShapeDtypeStruct((4,), jnp.int32),
+            jax.ShapeDtypeStruct((1, D), f32),
         ],
-        scratch_shapes=[pltpu.SemaphoreType.DMA((2,))],
+        scratch_shapes=[pltpu.SemaphoreType.DMA((12,))],
         compiler_params=pltpu.CompilerParams(vmem_limit_bytes=VMEM_BYTES),
         cost_estimate=pl.CostEstimate(flops=0, bytes_accessed=26_000_000, transcendentals=0),
         name="fetch",
-    )(at, pltpu.with_memory_space_constraint(w_in, pltpu.HBM), pltpu.with_memory_space_constraint(w_out, pltpu.HBM))
-
-
-def project_kernel(at_ref, head_ref, other_ref, *refs):
-    blocks, out_ref, (rows_ref, w_ref) = refs[:4], refs[4], refs[5:]
+    )(gain, *in_hbm)
+
+
+def project_kernel(head_ref, other_ref, *refs):
+    blocks, out_ref, (rows_ref, w_ref) = refs[:4], refs[6], refs[7:]
     for i in range(REQUESTS // ROWS):
         rows = slice(i * ROWS, (i + 1) * ROWS)
         rows_ref[2 * i * ROWS : (2 * i + 1) * ROWS, :] = head_ref[rows, :]
@@ -202,10 +198,10 @@
         ).astype(bf16)
 
 
-def project(at, head_out, other_head, blocks):
+def project(head_out, other_head, blocks, place, gain):
     return pl.pallas_call(
         project_kernel,
-        in_specs=[pl.BlockSpec(memory_space=pltpu.SMEM)] + [pl.BlockSpec(memory_space=pltpu.VMEM)] * 6,
+        in_specs=[pl.BlockSpec(memory_space=pltpu.VMEM)] * 8,
         out_specs=pl.BlockSpec(memory_space=pltpu.VMEM),
         out_shape=jax.ShapeDtypeStruct((2 * REQUESTS, 4 * COLUMNS), bf16),
         scratch_shapes=[
@@ -215,7 +211,7 @@
         compiler_params=pltpu.CompilerParams(vmem_limit_bytes=VMEM_BYTES),
         cost_estimate=pl.CostEstimate(flops=2 * REQUESTS * 512 * D, bytes_accessed=4_500_000, transcendentals=0),
         name="project",
-    )(at, head_out, other_head, *blocks)
+    )(head_out, other_head, *blocks, place, gain)
 
 
 def total_kernel(parts_ref, own_ref, other_ref):
@@ -237,15 +233,13 @@
     )(parts)
 
 
-def dispatch_kernel(
-    at_ref, own_ref, other_ref, res_ref, gain_ref, place_ref, hidden_ref, out_ref, norm_ref, sum_ref
-):
-    z, core = at_ref[0], at_ref[3]
+def dispatch_kernel(own_ref, other_ref, res_ref, gain_ref, place_ref, hidden_ref, out_ref, norm_ref, sum_ref):
+    z, core = lax.axis_index("z"), lax.axis_index("core")
     own, other = own_ref[...].astype(f32), other_ref[...].astype(f32)
     even = jnp.where(core == 0, own, other)
     odd = jnp.where(core == 0, other, own)
-    for step in range(4):
-        columns = slice(step * COLUMNS, (step + 1) * COLUMNS)
+    for i, step in enumerate(CHIPS):
+        columns = slice(i * COLUMNS, (i + 1) * COLUMNS)
         start = pl.multiple_of(lax.rem(z + step, 4) * QUARTER, 128)
         sum_ref[:, pl.ds(start, QUARTER)] = jnp.concatenate([even[:, columns], odd[:, columns]], axis=1)
     hidden = (res_ref[...].astype(f32) + sum_ref[...]).astype(bf16)
@@ -262,10 +256,9 @@
         out_ref[rows, :] = mm(place_ref[rows, :], norm_ref[...]).astype(bf16)
 
 
-def dispatch(at, own, other, residual, gain, place):
+def dispatch(own, other, residual, gain, place):
     return pl.pallas_call(
         dispatch_kernel,
-        in_specs=[pl.BlockSpec(memory_space=pltpu.SMEM)] + [pl.BlockSpec(memory_space=pltpu.VMEM)] * 5,
         out_shape=(
             jax.ShapeDtypeStruct((ROWS, D), bf16),
             jax.ShapeDtypeStruct((PIECES, QUARTER), bf16),
@@ -274,7 +267,7 @@
         compiler_params=pltpu.CompilerParams(vmem_limit_bytes=VMEM_BYTES),
         cost_estimate=pl.CostEstimate(flops=120_000_000, bytes_accessed=4_000_000, transcendentals=16),
         name="dispatch",
-    )(at, own, other, residual, gain, place)
+    )(own, other, residual, gain, place)
 
 
 def expert_kernel(x_ref, wi_ref, wo_ref, out_ref, rows_ref, act_ref, back_ref):
@@ -363,9 +356,7 @@
     w_down,
 ):
     own = out_proj.T
-    others = [lax.ppermute(own, "z", [(i, (i - step) % 4) for i in range(4)]) for step in (1, 2, 3)]
-    at = jnp.stack([lax.axis_index(name) for name in ("z", "y", "x", "core")]).astype(jnp.int32)
-
+    others = [lax.ppermute(own, "z", [(i, (i - step) % 4) for i in range(4)]) for step in CHIPS[1:]]
     def other_core(block):
         return lax.ppermute(block, "core", [(0, 1), (1, 0)])
 
@@ -375,14 +366,14 @@
         lengths.reshape(1, REQUESTS),
         value_up_weight,
     )
-    place, weight, gain, at = plan(at, routes, route_scores, norm_gain.reshape(1, D))
-    w_in, w_out, at = fetch(at, w_gate_up[0], w_down[0])
-    shares = project(at, head_out, other_core(head_out), (own, *others))
+    place, weight = plan(routes, route_scores)
+    w_in, w_out, gain = fetch(norm_gain.reshape(1, D), w_gate_up[0], w_down[0])
+    shares = project(head_out, other_core(head_out), (own, *others), place, gain)
     parts = lax.all_to_all(
         shares.reshape(16, 2 * ROWS, 4 * COLUMNS), ("y", "x"), split_axis=0, concat_axis=0, tiled=True
     )
     own_total, other_total = total(parts)
-    hidden, outgoing = dispatch(at, own_total, other_core(other_total), residual_in, gain, place)
+    hidden, outgoing = dispatch(own_total, other_core(other_total), residual_in, gain, place)
     everyone = ("z", "core", "y", "x")
     arrived = lax.all_to_all(
         outgoing.reshape(EXPERTS, 8, QUARTER), everyone, split_axis=0, concat_axis=0, tiled=True

time: 136 us -> 133 us (0.978)
  Pallas kernels: 28.4 us -> 25.7 us
  blocking collectives: 93.9 us -> 91.9 us
  waiting for transfers between devices: 0.9 us -> 2.73 us
    ppermute x3, waiting for transfers between devices: 0.01 us -> 1.83 us  [local(): lax.ppermute(own, 'z', [(i, (i - step) % 4) for i in range(4)])]
    all_to_all x1, blocking collectives: 31.8 us -> 30.2 us  [local(): lax.all_to_all(outgoing.reshape(EXPERTS, 8, QUARTER), everyone, split_axi...]
    pallas_call x2, Pallas kernels: 10.2 us -> 8.74 us  [the longest x1 7.48 us: fetch(): pl.pallas_call(fetch_kernel, in_specs=[pl.BlockSpec(memory_space=space) f...]
  transfers between devices with their start and end apart: 5 -> 5, of which waited for: 1 -> 2; matrix products, arithmetic and copies ran while one was open for 0% -> 0% of each run, Pallas kernels for 12% -> 11%
where the time goes in v4:
time: 133 us
  blocking collectives  91.9 us (69%)
  Pallas kernels  25.7 us (19%)
  starting transfers between devices  10.5 us (8%)
  waiting for transfers between devices  2.73 us (2%)
  local copies, waits for them, and re-layouts  1.76 us (1%)
    all_to_all x1, blocking collectives, local(): lax.all_to_all(produced.reshape(EXPERTS, 8, QUARTER), everyone, split_axi...  31.5 us
    all_to_all x1, blocking collectives, local(): lax.all_to_all(shares.reshape(16, 2 * ROWS, 4 * COLUMNS), ('y', 'x'), spl...  30.3 us
    all_to_all x1, blocking collectives, local(): lax.all_to_all(outgoing.reshape(EXPERTS, 8, QUARTER), everyone, split_axi...  30.2 us
    pallas_call x1, Pallas kernels, fetch(): pl.pallas_call(fetch_kernel, in_specs=[pl.BlockSpec(memory_space=space) f...  7.48 us
    pallas_call x1, Pallas kernels, expert(): pl.pallas_call(expert_kernel, in_specs=[pl.BlockSpec(memory_space=pltpu.V...  7.29 us
    pallas_call x1, Pallas kernels, attention(): pl.pallas_call(attention_kernel, grid=(REQUESTS // 128,), in_specs=[pl.Bl...  6.3 us
    ppermute x3, starting transfers between devices, local(): lax.ppermute(own, 'z', [(i, (i - step) % 4) for i in range(4)])  5.89 us
    ppermute x2, starting transfers between devices, other_core(): return lax.ppermute(block, 'core', [(0, 1), (1, 0)])  4.64 us
  transfers between devices with their start and end apart: 5, of which 2 were waited for; matrix products, arithmetic and copies ran while one was open for 0% of the time, Pallas kernels for 11%

profile of v4, /device:TPU:1, one launch (start us, length us, event | category | flops | bytes accessed | tf_op | source)
XLA Modules:
  0.0 132.8 jit_solution(8967334111985538693)
XLA Ops:
  0.0 2.5 %collective-permute-start.3 = (bf16[448,512]{1,0:T(8,128)(2,1)}, bf16[448,512]{1,0:T(8,128)(2,1)S(1)}, u32[]{:S(2)}, u32[]{:S(2)}) collective-permute-start(bf16[448,512]{1,0:T(8,128)(2,1)} %bitcast.18), channel_id=1, source_target_pairs={{0,32},{32,64},{64,96},{96,0},{1,33},{33,65},{65,97},{97,1},{2,34}... | collective-permute-start | bytes 1376264 | tf_op jit(solution)/shard_map/ppermute | solution.py:359
  2.5 2.1 %collective-permute-start.2 = (bf16[448,512]{1,0:T(8,128)(2,1)}, bf16[448,512]{1,0:T(8,128)(2,1)S(1)}, u32[]{:S(2)}, u32[]{:S(2)}) collective-permute-start(bf16[448,512]{1,0:T(8,128)(2,1)} %bitcast.19), channel_id=1, source_target_pairs={{0,96},{32,0},{64,32},{96,64},{1,97},{33,1},{65,33},{97,65},{2,98}... | collective-permute-start | bytes 1376264 | tf_op jit(solution)/shard_map/ppermute | solution.py:359
  4.6 1.3 collective-permute-start.1
  5.9 1.0 copy-done.2
  6.9 0.7 copy-done.5
  7.6 6.3 %attention.1.head_ref = bf16[256,512]{1,0:T(8,128)(2,1)S(1)} custom-call(bf16[4,576,256]{2,1,0:T(8,128)(2,1)} %bitcast.28, bf16[8,576,256]{2,1,0:T(8,128)(2,1)} %bitcast.27, s32[1,256]{1,0:T(1,128)S(1)} %bitcast.24, bf16[4,512,128]{2,1,0:T(8,128)(2,1)S(1)} %copy-done.2), custom_call_target="tpu_custom_call" | custom-call | flops 8999999488 | bytes 4200000 | tf_op jit(solution)/shard_map/attention/pallas_call | solution.py:80
  13.9 1.6 %collective-permute-start = (bf16[256,512]{1,0:T(8,128)(2,1)S(1)}, bf16[256,512]{1,0:T(8,128)(2,1)S(1)}, u32[]{:S(2)}, u32[]{:S(2)}) collective-permute-start(bf16[256,512]{1,0:T(8,128)(2,1)S(1)} %attention.1.head_ref), channel_id=1, source_target_pairs={{0,16},{16,0},{1,17},{17,1},{2,18},{18,2},{3,19},{19,3},{4,20},{20... | collective-permute-start | bytes 786440 | tf_op jit(solution)/shard_map/ppermute | solution.py:361
  15.5 0.0 copy-start.3
  15.6 0.0 copy-start.4
  15.6 0.0 copy-start
  15.6 7.5 %fetch.1 = (bf16[3584,2048]{1,0:T(8,128)(2,1)S(1)}, bf16[1024,3584]{1,0:T(8,128)(2,1)S(1)}, f32[1,3584]{1,0:T(1,128)S(1)}) custom-call(f32[1,3584]{1,0:T(1,128)S(1)} %reshape.22.gain_ref, bf16[3584,2048]{1,0:T(8,128)(2,1)} %bitcast.25, bf16[1024,3584]{1,0:T(8,128)(2,1)} %bitcast.26), custom_call_target="tpu_custom_call" | custom-call | bytes 26000000 | tf_op jit(solution)/shard_map/fetch/pallas_call | solution.py:170
  23.1 0.8 plan.1
  23.9 0.0 collective-permute-done.2.refs_2_
  23.9 1.8 %collective-permute-done.1.refs_1_ = bf16[448,512]{1,0:T(8,128)(2,1)S(1)} collective-permute-done((bf16[448,512]{1,0:T(8,128)(2,1)}, bf16[448,512]{1,0:T(8,128)(2,1)S(1)}, u32[]{:S(2)}, u32[]{:S(2)}) %collective-permute-start.1) | collective-permute-done | bytes 458784 | tf_op jit(solution)/shard_map/ppermute | solution.py:359
  25.7 1.3 project.1
  27.0 30.3 %all_to_all.15.parts_ref = bf16[16,32,1792]{2,1,0:T(8,128)(2,1)S(1)} all-to-all(bf16[16,32,1792]{2,1,0:T(8,128)(2,1)S(1)} %bitcast.15), channel_id=1, replica_groups=mesh['z'=4,'core'=2,'y'=4,'x'=4] {'y','x'}, dimensions={0} | all-to-all | bytes 3670016 | tf_op jit(solution)/shard_map/all_to_all | solution.py:372
  57.3 0.2 total.1
  57.5 3.0 %collective-permute-start.4 = (bf16[16,1792]{1,0:T(8,128)(2,1)S(1)}, bf16[16,1792]{1,0:T(8,128)(2,1)S(1)}, u32[]{:S(2)}, u32[]{:S(2)}) collective-permute-start(bf16[16,1792]{1,0:T(8,128)(2,1)S(1)} %get-tuple-element.17), channel_id=1, source_target_pairs={{0,16},{16,0},{1,17},{17,1},{2,18},{18,2},{3,19},{19,3},{4,20},{20... | collective-permute-start | bytes 172040 | tf_op jit(solution)/shard_map/ppermute | solution.py:361
  60.6 0.9 collective-permute-done.4.other_ref
  61.5 1.3 dispatch.1
  62.7 30.2 %all_to_all.16 = bf16[128,8,896]{2,1,0:T(8,128)(2,1)S(1)} all-to-all(bf16[128,8,896]{2,1,0:T(8,128)(2,1)S(1)} %bitcast.17), channel_id=1, replica_groups=mesh['z'=4,'core'=2,'y'=4,'x'=4] {'z','core','y','x'}, dimensions={0} | all-to-all | bytes 3670016 | tf_op jit(solution)/shard_map/all_to_all | solution.py:378
  92.9 7.3 %expert.1 = bf16[1024,896]{1,0:T(8,128)(2,1)S(1)} custom-call(bf16[1024,896]{1,0:T(8,128)(2,1)S(1)} %bitcast.13, bf16[3584,2048]{1,0:T(8,128)(2,1)S(1)} %get-tuple-element.19.wi_ref, bf16[1024,3584]{1,0:T(8,128)(2,1)S(1)} %get-tuple-element.20.wo_ref), custom_call_target="tpu_custom_call" | custom-call | flops 5637144576 | bytes 26000000 | tf_op jit(solution)/shard_map/expert/pallas_call | solution.py:304
  100.2 31.5 %all_to_all.17 = bf16[128,8,896]{2,1,0:T(8,128)(2,1)S(1)} all-to-all(bf16[128,8,896]{2,1,0:T(8,128)(2,1)S(1)} %bitcast.14), channel_id=1, replica_groups=mesh['z'=4,'core'=2,'y'=4,'x'=4] {'z','core','y','x'}, dimensions={0} | all-to-all | bytes 3670016 | tf_op jit(solution)/shard_map/all_to_all | solution.py:382
  131.7 1.1 combine.1
  (12 shorter events, 0.0 us)
Async XLA Ops:
  0.0 23.9 %collective-permute-start.3 = (bf16[448,512]{1,0:T(8,128)(2,1)}, bf16[448,512]{1,0:T(8,128)(2,1)S(1)}, u32[]{:S(2)}, u32[]{:S(2)}) collective-permute-start(bf16[448,512]{1,0:T(8,128)(2,1)} %bitcast.18), channel_id=1, source_target_pairs={{0,32},{32,64},{64,96},{96,0},{1,33},{33,65},{65,97},{97,1},{2,34}... | collective-permute-start | bytes 1376264 | tf_op jit(solution)/shard_map/ppermute | solution.py:359
  2.5 21.4 %collective-permute-start.2 = (bf16[448,512]{1,0:T(8,128)(2,1)}, bf16[448,512]{1,0:T(8,128)(2,1)S(1)}, u32[]{:S(2)}, u32[]{:S(2)}) collective-permute-start(bf16[448,512]{1,0:T(8,128)(2,1)} %bitcast.19), channel_id=1, source_target_pairs={{0,96},{32,0},{64,32},{96,64},{1,97},{33,1},{65,33},{97,65},{2,98}... | collective-permute-start | bytes 1376264 | tf_op jit(solution)/shard_map/ppermute | solution.py:359
  4.6 21.1 %collective-permute-start.1 = (bf16[448,512]{1,0:T(8,128)(2,1)}, bf16[448,512]{1,0:T(8,128)(2,1)S(1)}, u32[]{:S(2)}, u32[]{:S(2)}) collective-permute-start(bf16[448,512]{1,0:T(8,128)(2,1)} %bitcast.20), channel_id=1, source_target_pairs={{0,64},{32,96},{64,0},{96,32},{1,65},{33,97},{65,1},{97,33},{2,66}... | collective-permute-start | bytes 1376264 | tf_op jit(solution)/shard_map/ppermute | solution.py:359
  5.9 1.0 copy-start.2
  6.9 0.7 copy-start.5
  7.6 7.9 %copy-start.6 = (f32[3584]{0:T(1024)S(1)}, f32[3584]{0:T(1024)}, u32[]{:S(2)}) copy-start(f32[3584]{0:T(1024)} %param.17) | copy-start | bytes 43012
  13.9 9.9 %collective-permute-start = (bf16[256,512]{1,0:T(8,128)(2,1)S(1)}, bf16[256,512]{1,0:T(8,128)(2,1)S(1)}, u32[]{:S(2)}, u32[]{:S(2)}) collective-permute-start(bf16[256,512]{1,0:T(8,128)(2,1)S(1)} %attention.1.head_ref), channel_id=1, source_target_pairs={{0,16},{16,0},{1,17},{17,1},{2,18},{18,2},{3,19},{19,3},{4,20},{20... | collective-permute-start | bytes 786440 | tf_op jit(solution)/shard_map/ppermute | solution.py:361
  15.5 7.5 %copy-start.3 = (s32[16,8]{0,1:T(8,128)S(1)}, s32[16,8]{0,1:T(8,128)}, u32[]{:S(2)}) copy-start(s32[16,8]{0,1:T(8,128)} %param.18) | copy-start | bytes 1540
  15.6 7.5 %copy-start.4 = (f32[16,8]{0,1:T(8,128)S(1)}, f32[16,8]{0,1:T(8,128)}, u32[]{:S(2)}) copy-start(f32[16,8]{0,1:T(8,128)} %param.19) | copy-start | bytes 1540
  15.6 10.2 %copy-start = (bf16[512,448]{0,1:T(8,128)(2,1)S(1)}, bf16[512,448]{0,1:T(8,128)(2,1)}, u32[]{:S(2)}) copy-start(bf16[512,448]{0,1:T(8,128)(2,1)} %param.15) | copy-start | bytes 1376260
  57.3 4.2 %copy-start.1 = (bf16[16,3584]{1,0:T(8,128)(2,1)S(1)}, bf16[16,3584]{1,0:T(8,128)(2,1)}, u32[]{:S(2)}) copy-start(bf16[16,3584]{1,0:T(8,128)(2,1)} %res_ref.1) | copy-start | bytes 344068
  57.5 3.9 %collective-permute-start.4 = (bf16[16,1792]{1,0:T(8,128)(2,1)S(1)}, bf16[16,1792]{1,0:T(8,128)(2,1)S(1)}, u32[]{:S(2)}, u32[]{:S(2)}) collective-permute-start(bf16[16,1792]{1,0:T(8,128)(2,1)S(1)} %get-tuple-element.17), channel_id=1, source_target_pairs={{0,16},{16,0},{1,17},{17,1},{2,18},{18,2},{3,19},{19,3},{4,20},{20... | collective-permute-start | bytes 172040 | tf_op jit(solution)/shard_map/ppermute | solution.py:361

commit v5 on v4

--- a/solution.py
+++ b/solution.py
@@ -250,9 +250,8 @@
     for quarter in range(4):
         norm_ref[pl.ds(quarter * ROWS, ROWS), :] = normed[:, quarter * QUARTER : (quarter + 1) * QUARTER]
 
-    @pl.loop(0, 4)
-    def _(i):
-        rows = pl.ds(i * (PIECES // 4), PIECES // 4)
+    for start in range(0, PIECES, PIECES // 4):
+        rows = slice(start, start + PIECES // 4)
         out_ref[rows, :] = mm(place_ref[rows, :], norm_ref[...]).astype(bf16)
 
 
@@ -271,7 +270,7 @@
 
 
 def expert_kernel(x_ref, wi_ref, wo_ref, out_ref, rows_ref, act_ref, back_ref):
-    half = FF // 4
+    half = FF // 2
 
     def matches(to, frm):
         same_quarter = to // 64 == frm % 8 // 2
@@ -279,24 +278,35 @@
 
     sort = matches(iota((256, 256), 0), iota((256, 256), 1))
     unsort = matches(iota((256, 256), 1), iota((256, 256), 0))
-    for b in range(4):
-        sorted_rows = mm(sort, x_ref[b * 256 : (b + 1) * 256, :]).astype(bf16)
-        for quarter in range(4):
-            rows_ref[b * 64 : (b + 1) * 64, quarter * QUARTER : (quarter + 1) * QUARTER] = sorted_rows[
-                quarter * 64 : (quarter + 1) * 64
-            ]
-
-    for i in range(4):
+    for pair in range(2):
+        blocks = [x_ref[b * 256 : (b + 1) * 256, :] for b in (2 * pair, 2 * pair + 1)]
+        sorted_rows = mm(sort, jnp.concatenate(blocks, axis=1)).astype(bf16)
+        for i in range(2):
+            start = (2 * pair + i) * 64
+            for quarter in range(4):
+                rows_ref[start : start + 64, quarter * QUARTER : (quarter + 1) * QUARTER] = sorted_rows[
+                    quarter * 64 : (quarter + 1) * 64, i * QUARTER : (i + 1) * QUARTER
+                ]
+
+    for i in range(2):
         gate = mm(rows_ref[...], wi_ref[:, i * half : (i + 1) * half])
         up = mm(rows_ref[...], wi_ref[:, FF + i * half : FF + (i + 1) * half])
         act_ref[:, i * half : (i + 1) * half] = (jax.nn.silu(gate) * up).astype(bf16)
 
-    for quarter in range(4):
-        result = mm(act_ref[...], wo_ref[:, quarter * QUARTER : (quarter + 1) * QUARTER]).astype(bf16)
-        for b in range(4):
-            back_ref[b, quarter * 64 : (quarter + 1) * 64, :] = result[b * 64 : (b + 1) * 64]
-    for b in range(4):
-        out_ref[b * 256 : (b + 1) * 256, :] = mm(unsort, back_ref[b]).astype(bf16)
+    for pair in range(2):
+        result = mm(act_ref[...], wo_ref[:, pair * 2 * QUARTER : (pair + 1) * 2 * QUARTER]).astype(bf16)
+        for i in range(2):
+            rows = slice((2 * pair + i) * 64, (2 * pair + i + 1) * 64)
+            for b in range(4):
+                columns = slice(b % 2 * QUARTER, (b % 2 + 1) * QUARTER)
+                back_ref[b // 2, rows, columns] = result[
+                    b * 64 : (b + 1) * 64, i * QUARTER : (i + 1) * QUARTER
+                ]
+    for pair in range(2):
+        result = mm(unsort, back_ref[pair]).astype(bf16)
+        for i in range(2):
+            start = (2 * pair + i) * 256
+            out_ref[start : start + 256, :] = result[:, i * QUARTER : (i + 1) * QUARTER]
 
 
 def expert(pieces, w_in, w_out):
@@ -309,7 +319,7 @@
         scratch_shapes=[
             pltpu.VMEM((rows, D), bf16),
             pltpu.VMEM((rows, FF), bf16),
-            pltpu.VMEM((4, 256, QUARTER), bf16),
+            pltpu.VMEM((2, 256, 2 * QUARTER), bf16),
         ],
         compiler_params=pltpu.CompilerParams(vmem_limit_bytes=VMEM_BYTES),
         cost_estimate=pl.CostEstimate(

time: 133 us -> 132 us (level)
  no operation moved by 1% of the time
where the time goes in v5:
time: 132 us
  blocking collectives  92 us (70%)
  Pallas kernels  25 us (19%)
  starting transfers between devices  10.5 us (8%)
  waiting for transfers between devices  2.73 us (2%)
  local copies, waits for them, and re-layouts  1.76 us (1%)
    all_to_all x1, blocking collectives, local(): lax.all_to_all(produced.reshape(EXPERTS, 8, QUARTER), everyone, split_axi...  31.5 us
    all_to_all x1, blocking collectives, local(): lax.all_to_all(shares.reshape(16, 2 * ROWS, 4 * COLUMNS), ('y', 'x'), spl...  30.3 us
    all_to_all x1, blocking collectives, local(): lax.all_to_all(outgoing.reshape(EXPERTS, 8, QUARTER), everyone, split_axi...  30.2 us
    pallas_call x1, Pallas kernels, fetch(): pl.pallas_call(fetch_kernel, in_specs=[pl.BlockSpec(memory_space=space) f...  7.48 us
    pallas_call x1, Pallas kernels, expert(): pl.pallas_call(expert_kernel, in_specs=[pl.BlockSpec(memory_space=pltpu.V...  6.93 us
    pallas_call x1, Pallas kernels, attention(): pl.pallas_call(attention_kernel, grid=(REQUESTS // 128,), in_specs=[pl.Bl...  6.3 us
    ppermute x3, starting transfers between devices, local(): lax.ppermute(own, 'z', [(i, (i - step) % 4) for i in range(4)])  5.89 us
    ppermute x2, starting transfers between devices, other_core(): return lax.ppermute(block, 'core', [(0, 1), (1, 0)])  4.64 us
  transfers between devices with their start and end apart: 5, of which 2 were waited for; matrix products, arithmetic and copies ran while one was open for 0% of the time, Pallas kernels for 11%

profile of v5, /device:TPU:1, one launch (start us, length us, event | category | flops | bytes accessed | tf_op | source)
XLA Modules:
  0.0 132.0 jit_solution(11313632969934454702)
XLA Ops:
  0.0 2.5 %collective-permute-start.3 = (bf16[448,512]{1,0:T(8,128)(2,1)}, bf16[448,512]{1,0:T(8,128)(2,1)S(1)}, u32[]{:S(2)}, u32[]{:S(2)}) collective-permute-start(bf16[448,512]{1,0:T(8,128)(2,1)} %bitcast.18), channel_id=1, source_target_pairs={{0,32},{32,64},{64,96},{96,0},{1,33},{33,65},{65,97},{97,1},{2,34}... | collective-permute-start | bytes 1376264 | tf_op jit(solution)/shard_map/ppermute | solution.py:369
  2.5 2.1 %collective-permute-start.2 = (bf16[448,512]{1,0:T(8,128)(2,1)}, bf16[448,512]{1,0:T(8,128)(2,1)S(1)}, u32[]{:S(2)}, u32[]{:S(2)}) collective-permute-start(bf16[448,512]{1,0:T(8,128)(2,1)} %bitcast.19), channel_id=1, source_target_pairs={{0,96},{32,0},{64,32},{96,64},{1,97},{33,1},{65,33},{97,65},{2,98}... | collective-permute-start | bytes 1376264 | tf_op jit(solution)/shard_map/ppermute | solution.py:369
  4.6 1.3 collective-permute-start.1
  5.9 1.0 copy-done.2
  6.9 0.7 copy-done.5
  7.6 6.3 %attention.1.head_ref = bf16[256,512]{1,0:T(8,128)(2,1)S(1)} custom-call(bf16[4,576,256]{2,1,0:T(8,128)(2,1)} %bitcast.28, bf16[8,576,256]{2,1,0:T(8,128)(2,1)} %bitcast.27, s32[1,256]{1,0:T(1,128)S(1)} %bitcast.24, bf16[4,512,128]{2,1,0:T(8,128)(2,1)S(1)} %copy-done.2), custom_call_target="tpu_custom_call" | custom-call | flops 8999999488 | bytes 4200000 | tf_op jit(solution)/shard_map/attention/pallas_call | solution.py:80
  13.9 1.6 %collective-permute-start = (bf16[256,512]{1,0:T(8,128)(2,1)S(1)}, bf16[256,512]{1,0:T(8,128)(2,1)S(1)}, u32[]{:S(2)}, u32[]{:S(2)}) collective-permute-start(bf16[256,512]{1,0:T(8,128)(2,1)S(1)} %attention.1.head_ref), channel_id=1, source_target_pairs={{0,16},{16,0},{1,17},{17,1},{2,18},{18,2},{3,19},{19,3},{4,20},{20... | collective-permute-start | bytes 786440 | tf_op jit(solution)/shard_map/ppermute | solution.py:371
  15.5 0.0 copy-start.3
  15.6 0.0 copy-start.4
  15.6 0.0 copy-start
  15.6 7.5 %fetch.1 = (bf16[3584,2048]{1,0:T(8,128)(2,1)S(1)}, bf16[1024,3584]{1,0:T(8,128)(2,1)S(1)}, f32[1,3584]{1,0:T(1,128)S(1)}) custom-call(f32[1,3584]{1,0:T(1,128)S(1)} %reshape.22.gain_ref, bf16[3584,2048]{1,0:T(8,128)(2,1)} %bitcast.25, bf16[1024,3584]{1,0:T(8,128)(2,1)} %bitcast.26), custom_call_target="tpu_custom_call" | custom-call | bytes 26000000 | tf_op jit(solution)/shard_map/fetch/pallas_call | solution.py:170
  23.1 0.8 plan.1
  23.9 0.0 collective-permute-done.other_ref
  23.9 1.8 %collective-permute-done.1.refs_1_ = bf16[448,512]{1,0:T(8,128)(2,1)S(1)} collective-permute-done((bf16[448,512]{1,0:T(8,128)(2,1)}, bf16[448,512]{1,0:T(8,128)(2,1)S(1)}, u32[]{:S(2)}, u32[]{:S(2)}) %collective-permute-start.1) | collective-permute-done | bytes 458784 | tf_op jit(solution)/shard_map/ppermute | solution.py:369
  25.7 1.3 project.1
  27.0 30.3 %all_to_all.15.parts_ref = bf16[16,32,1792]{2,1,0:T(8,128)(2,1)S(1)} all-to-all(bf16[16,32,1792]{2,1,0:T(8,128)(2,1)S(1)} %bitcast.15), channel_id=1, replica_groups=mesh['z'=4,'core'=2,'y'=4,'x'=4] {'y','x'}, dimensions={0} | all-to-all | bytes 3670016 | tf_op jit(solution)/shard_map/all_to_all | solution.py:382
  57.3 0.2 total.1
  57.5 3.0 %collective-permute-start.4 = (bf16[16,1792]{1,0:T(8,128)(2,1)S(1)}, bf16[16,1792]{1,0:T(8,128)(2,1)S(1)}, u32[]{:S(2)}, u32[]{:S(2)}) collective-permute-start(bf16[16,1792]{1,0:T(8,128)(2,1)S(1)} %get-tuple-element.17), channel_id=1, source_target_pairs={{0,16},{16,0},{1,17},{17,1},{2,18},{18,2},{3,19},{19,3},{4,20},{20... | collective-permute-start | bytes 172040 | tf_op jit(solution)/shard_map/ppermute | solution.py:371
  60.6 0.9 collective-permute-done.4.other_ref
  61.5 0.8 dispatch.1
  62.3 30.2 %all_to_all.16 = bf16[128,8,896]{2,1,0:T(8,128)(2,1)S(1)} all-to-all(bf16[128,8,896]{2,1,0:T(8,128)(2,1)S(1)} %bitcast.17), channel_id=1, replica_groups=mesh['z'=4,'core'=2,'y'=4,'x'=4] {'z','core','y','x'}, dimensions={0} | all-to-all | bytes 3670016 | tf_op jit(solution)/shard_map/all_to_all | solution.py:388
  92.5 6.9 %expert.1 = bf16[1024,896]{1,0:T(8,128)(2,1)S(1)} custom-call(bf16[1024,896]{1,0:T(8,128)(2,1)S(1)} %bitcast.13, bf16[3584,2048]{1,0:T(8,128)(2,1)S(1)} %get-tuple-element.19.wi_ref, bf16[1024,3584]{1,0:T(8,128)(2,1)S(1)} %get-tuple-element.20.wo_ref), custom_call_target="tpu_custom_call" | custom-call | flops 5637144576 | bytes 26000000 | tf_op jit(solution)/shard_map/expert/pallas_call | solution.py:314
  99.5 31.5 %all_to_all.17 = bf16[128,8,896]{2,1,0:T(8,128)(2,1)S(1)} all-to-all(bf16[128,8,896]{2,1,0:T(8,128)(2,1)S(1)} %bitcast.14), channel_id=1, replica_groups=mesh['z'=4,'core'=2,'y'=4,'x'=4] {'z','core','y','x'}, dimensions={0} | all-to-all | bytes 3670016 | tf_op jit(solution)/shard_map/all_to_all | solution.py:392
  130.9 1.1 combine.1
  (12 shorter events, 0.0 us)
Async XLA Ops:
  0.0 23.9 %collective-permute-start.3 = (bf16[448,512]{1,0:T(8,128)(2,1)}, bf16[448,512]{1,0:T(8,128)(2,1)S(1)}, u32[]{:S(2)}, u32[]{:S(2)}) collective-permute-start(bf16[448,512]{1,0:T(8,128)(2,1)} %bitcast.18), channel_id=1, source_target_pairs={{0,32},{32,64},{64,96},{96,0},{1,33},{33,65},{65,97},{97,1},{2,34}... | collective-permute-start | bytes 1376264 | tf_op jit(solution)/shard_map/ppermute | solution.py:369
  2.5 21.4 %collective-permute-start.2 = (bf16[448,512]{1,0:T(8,128)(2,1)}, bf16[448,512]{1,0:T(8,128)(2,1)S(1)}, u32[]{:S(2)}, u32[]{:S(2)}) collective-permute-start(bf16[448,512]{1,0:T(8,128)(2,1)} %bitcast.19), channel_id=1, source_target_pairs={{0,96},{32,0},{64,32},{96,64},{1,97},{33,1},{65,33},{97,65},{2,98}... | collective-permute-start | bytes 1376264 | tf_op jit(solution)/shard_map/ppermute | solution.py:369
  4.6 21.1 %collective-permute-start.1 = (bf16[448,512]{1,0:T(8,128)(2,1)}, bf16[448,512]{1,0:T(8,128)(2,1)S(1)}, u32[]{:S(2)}, u32[]{:S(2)}) collective-permute-start(bf16[448,512]{1,0:T(8,128)(2,1)} %bitcast.20), channel_id=1, source_target_pairs={{0,64},{32,96},{64,0},{96,32},{1,65},{33,97},{65,1},{97,33},{2,66}... | collective-permute-start | bytes 1376264 | tf_op jit(solution)/shard_map/ppermute | solution.py:369
  5.9 1.0 copy-start.2
  6.9 0.7 copy-start.5
  7.6 7.9 %copy-start.6 = (f32[3584]{0:T(1024)S(1)}, f32[3584]{0:T(1024)}, u32[]{:S(2)}) copy-start(f32[3584]{0:T(1024)} %param.17) | copy-start | bytes 43012
  13.9 9.9 %collective-permute-start = (bf16[256,512]{1,0:T(8,128)(2,1)S(1)}, bf16[256,512]{1,0:T(8,128)(2,1)S(1)}, u32[]{:S(2)}, u32[]{:S(2)}) collective-permute-start(bf16[256,512]{1,0:T(8,128)(2,1)S(1)} %attention.1.head_ref), channel_id=1, source_target_pairs={{0,16},{16,0},{1,17},{17,1},{2,18},{18,2},{3,19},{19,3},{4,20},{20... | collective-permute-start | bytes 786440 | tf_op jit(solution)/shard_map/ppermute | solution.py:371
  15.5 7.5 %copy-start.3 = (s32[16,8]{0,1:T(8,128)S(1)}, s32[16,8]{0,1:T(8,128)}, u32[]{:S(2)}) copy-start(s32[16,8]{0,1:T(8,128)} %param.18) | copy-start | bytes 1540
  15.6 7.5 %copy-start.4 = (f32[16,8]{0,1:T(8,128)S(1)}, f32[16,8]{0,1:T(8,128)}, u32[]{:S(2)}) copy-start(f32[16,8]{0,1:T(8,128)} %param.19) | copy-start | bytes 1540
  15.6 10.2 %copy-start = (bf16[512,448]{0,1:T(8,128)(2,1)S(1)}, bf16[512,448]{0,1:T(8,128)(2,1)}, u32[]{:S(2)}) copy-start(bf16[512,448]{0,1:T(8,128)(2,1)} %param.15) | copy-start | bytes 1376260
  57.3 4.2 %copy-start.1 = (bf16[16,3584]{1,0:T(8,128)(2,1)S(1)}, bf16[16,3584]{1,0:T(8,128)(2,1)}, u32[]{:S(2)}) copy-start(bf16[16,3584]{1,0:T(8,128)(2,1)} %res_ref.1) | copy-start | bytes 344068
  57.5 3.9 %collective-permute-start.4 = (bf16[16,1792]{1,0:T(8,128)(2,1)S(1)}, bf16[16,1792]{1,0:T(8,128)(2,1)S(1)}, u32[]{:S(2)}, u32[]{:S(2)}) collective-permute-start(bf16[16,1792]{1,0:T(8,128)(2,1)S(1)} %get-tuple-element.17), channel_id=1, source_target_pairs={{0,16},{16,0},{1,17},{17,1},{2,18},{18,2},{3,19},{19,3},{4,20},{20... | collective-permute-start | bytes 172040 | tf_op jit(solution)/shard_map/ppermute | solution.py:371

commit v6 on v5

--- a/solution.py
+++ b/solution.py
@@ -100,7 +100,14 @@
     )
 
 
-def plan_kernel(routes_ref, score_ref, place_ref, weight_ref):
+def plan_kernel(routes_ref, score_ref, place_ref, weight_ref, sort_ref, unsort_ref):
+    def matches(to, frm):
+        same_quarter = to // 64 == frm % 8 // 2
+        return (same_quarter & (to % 64 // 2 == frm // 8) & (to % 2 == frm % 2)).astype(bf16)
+
+    sort_ref[...] = matches(iota((256, 256), 0), iota((256, 256), 1))
+    unsort_ref[...] = matches(iota((256, 256), 1), iota((256, 256), 0))
+
     routes, scores = routes_ref[...], score_ref[...]
     gates = 2.5 * scores / jnp.sum(scores, axis=0, keepdims=True)
     named = jnp.zeros((EXPERTS, ROWS), f32)
@@ -144,6 +151,8 @@
         out_shape=(
             jax.ShapeDtypeStruct((PIECES, 4 * ROWS), bf16),
             jax.ShapeDtypeStruct((8 * ROWS, PIECES), bf16),
+            jax.ShapeDtypeStruct((256, 256), bf16),
+            jax.ShapeDtypeStruct((256, 256), bf16),
         ),
         compiler_params=pltpu.CompilerParams(vmem_limit_bytes=VMEM_BYTES),
         cost_estimate=pl.CostEstimate(flops=60_000_000, bytes_accessed=500_000, transcendentals=0),
@@ -269,18 +278,12 @@
     )(own, other, residual, gain, place)
 
 
-def expert_kernel(x_ref, wi_ref, wo_ref, out_ref, rows_ref, act_ref, back_ref):
+def expert_kernel(x_ref, wi_ref, wo_ref, sort_ref, unsort_ref, out_ref, rows_ref, act_ref, back_ref):
     half = FF // 2
 
-    def matches(to, frm):
-        same_quarter = to // 64 == frm % 8 // 2
-        return (same_quarter & (to % 64 // 2 == frm // 8) & (to % 2 == frm % 2)).astype(bf16)
-
-    sort = matches(iota((256, 256), 0), iota((256, 256), 1))
-    unsort = matches(iota((256, 256), 1), iota((256, 256), 0))
     for pair in range(2):
         blocks = [x_ref[b * 256 : (b + 1) * 256, :] for b in (2 * pair, 2 * pair + 1)]
-        sorted_rows = mm(sort, jnp.concatenate(blocks, axis=1)).astype(bf16)
+        sorted_rows = mm(sort_ref[...], jnp.concatenate(blocks, axis=1)).astype(bf16)
         for i in range(2):
             start = (2 * pair + i) * 64
             for quarter in range(4):
@@ -303,17 +306,17 @@
                     b * 64 : (b + 1) * 64, i * QUARTER : (i + 1) * QUARTER
                 ]
     for pair in range(2):
-        result = mm(unsort, back_ref[pair]).astype(bf16)
+        result = mm(unsort_ref[...], back_ref[pair]).astype(bf16)
         for i in range(2):
             start = (2 * pair + i) * 256
             out_ref[start : start + 256, :] = result[:, i * QUARTER : (i + 1) * QUARTER]
 
 
-def expert(pieces, w_in, w_out):
+def expert(pieces, w_in, w_out, sort, unsort):
     rows = 2 * EXPERTS
     return pl.pallas_call(
         expert_kernel,
-        in_specs=[pl.BlockSpec(memory_space=pltpu.VMEM)] * 3,
+        in_specs=[pl.BlockSpec(memory_space=pltpu.VMEM)] * 5,
         out_specs=pl.BlockSpec(memory_space=pltpu.VMEM),
         out_shape=jax.ShapeDtypeStruct((PIECES, QUARTER), bf16),
         scratch_shapes=[
@@ -330,6 +333,8 @@
         pieces,
         w_in,
         w_out,
+        sort,
+        unsort,
     )
 
 
@@ -376,7 +381,7 @@
         lengths.reshape(1, REQUESTS),
         value_up_weight,
     )
-    place, weight = plan(routes, route_scores)
+    place, weight, sort, unsort = plan(routes, route_scores)
     w_in, w_out, gain = fetch(norm_gain.reshape(1, D), w_gate_up[0], w_down[0])
     shares = project(head_out, other_core(head_out), (own, *others), place, gain)
     parts = lax.all_to_all(
@@ -388,7 +393,7 @@
     arrived = lax.all_to_all(
         outgoing.reshape(EXPERTS, 8, QUARTER), everyone, split_axis=0, concat_axis=0, tiled=True
     )
-    produced = expert(arrived.reshape(PIECES, QUARTER), w_in, w_out)
+    produced = expert(arrived.reshape(PIECES, QUARTER), w_in, w_out, sort, unsort)
     returned = lax.all_to_all(
         produced.reshape(EXPERTS, 8, QUARTER), everyone, split_axis=0, concat_axis=0, tiled=True
     )

time: 132 us -> 132 us (level)
  no operation moved by 1% of the time
where the time goes in v6:
time: 132 us
  blocking collectives  92 us (70%)
  Pallas kernels  25 us (19%)
  starting transfers between devices  10.5 us (8%)
  waiting for transfers between devices  2.61 us (2%)
  local copies, waits for them, and re-layouts  1.76 us (1%)
    all_to_all x1, blocking collectives, local(): lax.all_to_all(produced.reshape(EXPERTS, 8, QUARTER), everyone, split_axi...  31.5 us
    all_to_all x1, blocking collectives, local(): lax.all_to_all(shares.reshape(16, 2 * ROWS, 4 * COLUMNS), ('y', 'x'), spl...  30.3 us
    all_to_all x1, blocking collectives, local(): lax.all_to_all(outgoing.reshape(EXPERTS, 8, QUARTER), everyone, split_axi...  30.2 us
    pallas_call x1, Pallas kernels, fetch(): pl.pallas_call(fetch_kernel, in_specs=[pl.BlockSpec(memory_space=space) f...  7.48 us
    pallas_call x1, Pallas kernels, expert(): pl.pallas_call(expert_kernel, in_specs=[pl.BlockSpec(memory_space=pltpu.V...  6.87 us
    pallas_call x1, Pallas kernels, attention(): pl.pallas_call(attention_kernel, grid=(REQUESTS // 128,), in_specs=[pl.Bl...  6.3 us
    ppermute x3, starting transfers between devices, local(): lax.ppermute(own, 'z', [(i, (i - step) % 4) for i in range(4)])  5.89 us
    ppermute x2, starting transfers between devices, other_core(): return lax.ppermute(block, 'core', [(0, 1), (1, 0)])  4.64 us
  transfers between devices with their start and end apart: 5, of which 2 were waited for; matrix products, arithmetic and copies ran while one was open for 0% of the time, Pallas kernels for 11%

profile of v6, /device:TPU:1, one launch (start us, length us, event | category | flops | bytes accessed | tf_op | source)
XLA Modules:
  0.0 132.0 jit_solution(7894351826853452159)
XLA Ops:
  0.0 2.5 %collective-permute-start.3 = (bf16[448,512]{1,0:T(8,128)(2,1)}, bf16[448,512]{1,0:T(8,128)(2,1)S(1)}, u32[]{:S(2)}, u32[]{:S(2)}) collective-permute-start(bf16[448,512]{1,0:T(8,128)(2,1)} %bitcast.18), channel_id=1, source_target_pairs={{0,32},{32,64},{64,96},{96,0},{1,33},{33,65},{65,97},{97,1},{2,34}... | collective-permute-start | bytes 1376264 | tf_op jit(solution)/shard_map/ppermute | solution.py:374
  2.5 2.1 %collective-permute-start.2 = (bf16[448,512]{1,0:T(8,128)(2,1)}, bf16[448,512]{1,0:T(8,128)(2,1)S(1)}, u32[]{:S(2)}, u32[]{:S(2)}) collective-permute-start(bf16[448,512]{1,0:T(8,128)(2,1)} %bitcast.19), channel_id=1, source_target_pairs={{0,96},{32,0},{64,32},{96,64},{1,97},{33,1},{65,33},{97,65},{2,98}... | collective-permute-start | bytes 1376264 | tf_op jit(solution)/shard_map/ppermute | solution.py:374
  4.6 1.3 collective-permute-start.1
  5.9 1.0 copy-done.2
  6.9 0.7 copy-done.5
  7.6 6.3 %attention.1.head_ref = bf16[256,512]{1,0:T(8,128)(2,1)S(1)} custom-call(bf16[4,576,256]{2,1,0:T(8,128)(2,1)} %bitcast.28, bf16[8,576,256]{2,1,0:T(8,128)(2,1)} %bitcast.27, s32[1,256]{1,0:T(1,128)S(1)} %bitcast.24, bf16[4,512,128]{2,1,0:T(8,128)(2,1)S(1)} %copy-done.2), custom_call_target="tpu_custom_call" | custom-call | flops 8999999488 | bytes 4200000 | tf_op jit(solution)/shard_map/attention/pallas_call | solution.py:80
  13.9 1.6 %collective-permute-start = (bf16[256,512]{1,0:T(8,128)(2,1)S(1)}, bf16[256,512]{1,0:T(8,128)(2,1)S(1)}, u32[]{:S(2)}, u32[]{:S(2)}) collective-permute-start(bf16[256,512]{1,0:T(8,128)(2,1)S(1)} %attention.1.head_ref), channel_id=1, source_target_pairs={{0,16},{16,0},{1,17},{17,1},{2,18},{18,2},{3,19},{19,3},{4,20},{20... | collective-permute-start | bytes 786440 | tf_op jit(solution)/shard_map/ppermute | solution.py:376
  15.5 0.0 copy-start.3
  15.6 0.0 copy-start.4
  15.6 0.0 copy-start
  15.6 7.5 %fetch.1 = (bf16[3584,2048]{1,0:T(8,128)(2,1)S(1)}, bf16[1024,3584]{1,0:T(8,128)(2,1)S(1)}, f32[1,3584]{1,0:T(1,128)S(1)}) custom-call(f32[1,3584]{1,0:T(1,128)S(1)} %reshape.22.gain_ref, bf16[3584,2048]{1,0:T(8,128)(2,1)} %bitcast.25, bf16[1024,3584]{1,0:T(8,128)(2,1)} %bitcast.26), custom_call_target="tpu_custom_call" | custom-call | bytes 26000000 | tf_op jit(solution)/shard_map/fetch/pallas_call | solution.py:179
  23.1 0.9 plan.1
  24.0 0.0 collective-permute-done.other_ref
  24.0 1.7 %collective-permute-done.1.refs_1_ = bf16[448,512]{1,0:T(8,128)(2,1)S(1)} collective-permute-done((bf16[448,512]{1,0:T(8,128)(2,1)}, bf16[448,512]{1,0:T(8,128)(2,1)S(1)}, u32[]{:S(2)}, u32[]{:S(2)}) %collective-permute-start.1) | collective-permute-done | bytes 458784 | tf_op jit(solution)/shard_map/ppermute | solution.py:374
  25.7 1.3 project.1
  27.0 30.3 %all_to_all.15.parts_ref = bf16[16,32,1792]{2,1,0:T(8,128)(2,1)S(1)} all-to-all(bf16[16,32,1792]{2,1,0:T(8,128)(2,1)S(1)} %bitcast.15), channel_id=1, replica_groups=mesh['z'=4,'core'=2,'y'=4,'x'=4] {'y','x'}, dimensions={0} | all-to-all | bytes 3670016 | tf_op jit(solution)/shard_map/all_to_all | solution.py:387
  57.3 0.2 total.1
  57.5 3.0 %collective-permute-start.4 = (bf16[16,1792]{1,0:T(8,128)(2,1)S(1)}, bf16[16,1792]{1,0:T(8,128)(2,1)S(1)}, u32[]{:S(2)}, u32[]{:S(2)}) collective-permute-start(bf16[16,1792]{1,0:T(8,128)(2,1)S(1)} %get-tuple-element.19), channel_id=1, source_target_pairs={{0,16},{16,0},{1,17},{17,1},{2,18},{18,2},{3,19},{19,3},{4,20},{20... | collective-permute-start | bytes 172040 | tf_op jit(solution)/shard_map/ppermute | solution.py:376
  60.6 0.9 collective-permute-done.4.other_ref
  61.5 0.8 dispatch.1
  62.3 30.2 %all_to_all.16 = bf16[128,8,896]{2,1,0:T(8,128)(2,1)S(1)} all-to-all(bf16[128,8,896]{2,1,0:T(8,128)(2,1)S(1)} %bitcast.17), channel_id=1, replica_groups=mesh['z'=4,'core'=2,'y'=4,'x'=4] {'z','core','y','x'}, dimensions={0} | all-to-all | bytes 3670016 | tf_op jit(solution)/shard_map/all_to_all | solution.py:393
  92.5 6.9 %expert.1 = bf16[1024,896]{1,0:T(8,128)(2,1)S(1)} custom-call(bf16[1024,896]{1,0:T(8,128)(2,1)S(1)} %bitcast.13, bf16[3584,2048]{1,0:T(8,128)(2,1)S(1)} %get-tuple-element.21.wi_ref, bf16[1024,3584]{1,0:T(8,128)(2,1)S(1)} %get-tuple-element.22.wo_ref, bf16[256,256]{1,0:T(8,128)(2,1)S(1)} %get-tuple-element.23.sort_ref, ...), custom_call_target="tpu_custom_call" | custom-call | flops 5637144576 | bytes 26000000 | tf_op jit(solution)/shard_map/expert/pallas_call | solution.py:317
  99.4 31.5 %all_to_all.17 = bf16[128,8,896]{2,1,0:T(8,128)(2,1)S(1)} all-to-all(bf16[128,8,896]{2,1,0:T(8,128)(2,1)S(1)} %bitcast.14), channel_id=1, replica_groups=mesh['z'=4,'core'=2,'y'=4,'x'=4] {'z','core','y','x'}, dimensions={0} | all-to-all | bytes 3670016 | tf_op jit(solution)/shard_map/all_to_all | solution.py:397
  130.9 1.1 combine.1
  (12 shorter events, 0.0 us)
Async XLA Ops:
  0.0 24.0 %collective-permute-start.3 = (bf16[448,512]{1,0:T(8,128)(2,1)}, bf16[448,512]{1,0:T(8,128)(2,1)S(1)}, u32[]{:S(2)}, u32[]{:S(2)}) collective-permute-start(bf16[448,512]{1,0:T(8,128)(2,1)} %bitcast.18), channel_id=1, source_target_pairs={{0,32},{32,64},{64,96},{96,0},{1,33},{33,65},{65,97},{97,1},{2,34}... | collective-permute-start | bytes 1376264 | tf_op jit(solution)/shard_map/ppermute | solution.py:374
  2.5 21.5 %collective-permute-start.2 = (bf16[448,512]{1,0:T(8,128)(2,1)}, bf16[448,512]{1,0:T(8,128)(2,1)S(1)}, u32[]{:S(2)}, u32[]{:S(2)}) collective-permute-start(bf16[448,512]{1,0:T(8,128)(2,1)} %bitcast.19), channel_id=1, source_target_pairs={{0,96},{32,0},{64,32},{96,64},{1,97},{33,1},{65,33},{97,65},{2,98}... | collective-permute-start | bytes 1376264 | tf_op jit(solution)/shard_map/ppermute | solution.py:374
  4.6 21.1 %collective-permute-start.1 = (bf16[448,512]{1,0:T(8,128)(2,1)}, bf16[448,512]{1,0:T(8,128)(2,1)S(1)}, u32[]{:S(2)}, u32[]{:S(2)}) collective-permute-start(bf16[448,512]{1,0:T(8,128)(2,1)} %bitcast.20), channel_id=1, source_target_pairs={{0,64},{32,96},{64,0},{96,32},{1,65},{33,97},{65,1},{97,33},{2,66}... | collective-permute-start | bytes 1376264 | tf_op jit(solution)/shard_map/ppermute | solution.py:374
  5.9 1.0 copy-start.2
  6.9 0.7 copy-start.5
  7.6 7.9 %copy-start.6 = (f32[3584]{0:T(1024)S(1)}, f32[3584]{0:T(1024)}, u32[]{:S(2)}) copy-start(f32[3584]{0:T(1024)} %param.17) | copy-start | bytes 43012
  13.9 10.1 %collective-permute-start = (bf16[256,512]{1,0:T(8,128)(2,1)S(1)}, bf16[256,512]{1,0:T(8,128)(2,1)S(1)}, u32[]{:S(2)}, u32[]{:S(2)}) collective-permute-start(bf16[256,512]{1,0:T(8,128)(2,1)S(1)} %attention.1.head_ref), channel_id=1, source_target_pairs={{0,16},{16,0},{1,17},{17,1},{2,18},{18,2},{3,19},{19,3},{4,20},{20... | collective-permute-start | bytes 786440 | tf_op jit(solution)/shard_map/ppermute | solution.py:376
  15.5 7.5 %copy-start.3 = (s32[16,8]{0,1:T(8,128)S(1)}, s32[16,8]{0,1:T(8,128)}, u32[]{:S(2)}) copy-start(s32[16,8]{0,1:T(8,128)} %param.18) | copy-start | bytes 1540
  15.6 7.5 %copy-start.4 = (f32[16,8]{0,1:T(8,128)S(1)}, f32[16,8]{0,1:T(8,128)}, u32[]{:S(2)}) copy-start(f32[16,8]{0,1:T(8,128)} %param.19) | copy-start | bytes 1540
  15.6 10.2 %copy-start = (bf16[512,448]{0,1:T(8,128)(2,1)S(1)}, bf16[512,448]{0,1:T(8,128)(2,1)}, u32[]{:S(2)}) copy-start(bf16[512,448]{0,1:T(8,128)(2,1)} %param.15) | copy-start | bytes 1376260
  57.3 4.2 %copy-start.1 = (bf16[16,3584]{1,0:T(8,128)(2,1)S(1)}, bf16[16,3584]{1,0:T(8,128)(2,1)}, u32[]{:S(2)}) copy-start(bf16[16,3584]{1,0:T(8,128)(2,1)} %res_ref.1) | copy-start | bytes 344068
  57.5 3.9 %collective-permute-start.4 = (bf16[16,1792]{1,0:T(8,128)(2,1)S(1)}, bf16[16,1792]{1,0:T(8,128)(2,1)S(1)}, u32[]{:S(2)}, u32[]{:S(2)}) collective-permute-start(bf16[16,1792]{1,0:T(8,128)(2,1)S(1)} %get-tuple-element.19), channel_id=1, source_target_pairs={{0,16},{16,0},{1,17},{17,1},{2,18},{18,2},{3,19},{19,3},{4,20},{20... | collective-permute-start | bytes 172040 | tf_op jit(solution)/shard_map/ppermute | solution.py:376
